TPU v7x, 32 devices: a whole 2x2x4 slice. The times are simulated.
32 devices in a mesh: kp: 8 (over y, x, core), ka: 4 (over z).
Axes of the slice: x: 2, y: 2, z: 4, core: 2. Of those that a mesh axis runs over, the one named last changes fastest.
Arguments:
- band_form: bfloat16 [16, 24, 2048], P('ka'), may hold values from -0.71875 to 0.71875
- interp_coef: bfloat16 [16, 128, 128], P('ka'), may hold values from -0.5 to 0.5
- screen: bfloat16 [16, 2048, 32], P('ka', 'kp'), may hold values from -0.3984375 to 0.3984375
- coulomb: float32 [2048], replicated, may hold values from 0.3 to 3
- shift_map: int32 [16, 2048], replicated, may hold values from 0 to 2047, each once within a row
- grid_order: int32 [16], replicated, may hold values from 0 to 15, each once
- energies: float32 [2048], P('ka'), may hold values from 0.09050967 to 0.271529
- initial: float32 [2048, 64], P('ka'), may hold values from -6 to 6
Outputs:
- kernel: bfloat16 [2048, 2048], P('ka', 'kp')
- subspace: float32 [2048, 64], P('ka')
All inputs are finite; a program needn't handle non-finite values.
Results may differ from a plain program's by a relative error of at most 0.02.
Values may be sent and summed in bfloat16 or wider, within the bound.
A program may use at most 64 MiB of HBM per device.

v0:
```python
import jax
import jax.numpy as jnp
from jax import lax
from jax.sharding import PartitionSpec as P

NV = 8
NC = 16
STEPS = 2
GRID_Y = 8


def broadcast(block, axis, source):
    block = jnp.where(lax.axis_index(axis) == source, block, jnp.zeros_like(block))
    return lax.psum(block, axis)


def pair_block(near_form, mapped, near_coef, far_coef, screen_cols, coulomb):
    valence = (
        (near_form[:NV, None, :].astype(jnp.float32) * mapped[None, :NV, :].astype(jnp.float32))
        .reshape(NV * NV, -1)
        .astype(jnp.bfloat16)
    )
    conduction = (
        (near_form[NV:, None, :].astype(jnp.float32) * mapped[None, NV:, :].astype(jnp.float32))
        .reshape(NC * NC, -1)
        .astype(jnp.bfloat16)
    )
    scaled = (coulomb[None, :] * valence.astype(jnp.float32)).astype(jnp.bfloat16)
    direct = jnp.dot(conduction, scaled.T, preferred_element_type=jnp.float32)
    left = jnp.dot(conduction, screen_cols, preferred_element_type=jnp.float32)
    right = jnp.dot(valence, screen_cols, preferred_element_type=jnp.float32)
    direct = direct + jnp.dot(
        left, right.T, precision=lax.Precision.HIGHEST, preferred_element_type=jnp.float32
    )
    block = (
        direct.reshape(NC, NC, NV, NV)
        .transpose(2, 0, 3, 1)
        .reshape(NV * NC, NV * NC)
        .astype(jnp.bfloat16)
    )
    half = jnp.dot(block, far_coef, preferred_element_type=jnp.float32).astype(jnp.bfloat16)
    return jnp.dot(near_coef.T, half, preferred_element_type=jnp.float32).astype(jnp.bfloat16)


def transfer_table(near_cells, far_cells, grid_x):
    step_x = (near_cells[:, None] // GRID_Y - far_cells[None, :] // GRID_Y) % grid_x
    step_y = (near_cells[:, None] % GRID_Y - far_cells[None, :] % GRID_Y) % GRID_Y
    return (step_x * GRID_Y + step_y).reshape(-1)


def on_device(band_form, interp_coef, screen, coulomb, shift_map, grid_order, energies, initial):
    size_ka = lax.axis_size("ka")
    size_kp = lax.axis_size("kp")
    tile_row = lax.axis_index("ka")
    tile_col = lax.axis_index("kp")
    near_count = band_form.shape[0]
    total_points = near_count * size_ka
    far_count = total_points // size_kp
    pairs = interp_coef.shape[1]
    grid_x = total_points // GRID_Y
    source_row = tile_col * far_count // near_count
    far_offset = tile_col * far_count % near_count
    far_form, far_coef = (
        broadcast(band_form, "ka", source_row),
        broadcast(interp_coef, "ka", source_row),
    )
    far_form = lax.dynamic_slice_in_dim(far_form, far_offset, far_count, 0)
    far_coef = lax.dynamic_slice_in_dim(far_coef, far_offset, far_count, 0)
    near_ids = tile_row * near_count + jnp.arange(near_count, dtype=jnp.int32)
    far_ids = tile_col * far_count + jnp.arange(far_count, dtype=jnp.int32)
    near_cells = jnp.take(grid_order, near_ids)
    far_cells = jnp.take(grid_order, far_ids)
    transfers = transfer_table(near_cells, far_cells, grid_x)
    column_ids = jnp.arange(size_kp * far_count, dtype=jnp.int32).reshape(size_kp, far_count)
    column_cells = jnp.take(grid_order, column_ids.reshape(-1)).reshape(size_kp, far_count)
    row_transfers = jax.vmap(lambda cells: transfer_table(near_cells, cells, grid_x))(column_cells)
    shard_piece = lax.all_gather(screen, "ka", axis=0, tiled=True)
    piece_rows = shard_piece.shape[0]
    matches = (
        row_transfers[:, :, None] == jnp.arange(piece_rows, dtype=jnp.int32)[None, None, :]
    ).astype(jnp.bfloat16)
    picked = jnp.einsum("cpn,nge->cpge", matches, shard_piece, preferred_element_type=jnp.float32)
    slices = picked.astype(jnp.bfloat16)
    pair_screen = lax.all_to_all(slices, "kp", split_axis=0, concat_axis=2, tiled=True)[0]
    near_slots = jnp.repeat(jnp.arange(near_count, dtype=jnp.int32), far_count)
    far_slots = jnp.tile(jnp.arange(far_count, dtype=jnp.int32), near_count)

    def one_pair(item):
        near_slot, far_slot, transfer, screen_cols = item
        mapping = shift_map[transfer]
        mapped = jnp.take(far_form[far_slot], mapping, axis=1)
        return pair_block(
            band_form[near_slot],
            mapped,
            interp_coef[near_slot],
            far_coef[far_slot],
            screen_cols,
            coulomb,
        )

    blocks = lax.map(one_pair, (near_slots, far_slots, transfers, pair_screen))
    kernel = (
        blocks.reshape(near_count, far_count, pairs, pairs)
        .transpose(0, 2, 1, 3)
        .reshape(near_count * pairs, far_count * pairs)
    )
    vectors = initial
    for repeat in range(STEPS):
        source_vectors = broadcast(vectors.astype(jnp.bfloat16), "ka", source_row)
        far_vectors = lax.dynamic_slice_in_dim(
            source_vectors, far_offset * pairs, far_count * pairs, 0
        )
        product = jnp.dot(kernel, far_vectors, preferred_element_type=jnp.float32)
        images = energies[:, None] * vectors + lax.psum(product, "kp")
        local_correlation = jnp.dot(
            images.T, images, precision=lax.Precision.HIGHEST, preferred_element_type=jnp.float32
        )
        correlation = lax.psum(local_correlation, "ka") / (total_points * pairs)
        factor = jnp.linalg.cholesky(correlation)
        vectors = jax.scipy.linalg.solve_triangular(factor, images.T, lower=True).T
    return (kernel, vectors)


def solution(mesh):
    return jax.shard_map(
        on_device,
        mesh=mesh,
        in_specs=(
            P("ka", None, None),
            P("ka", None, None),
            P("ka", "kp", None),
            P(),
            P(),
            P(),
            P("ka"),
            P("ka", None),
        ),
        out_specs=(P("ka", "kp"), P("ka", None)),
        check_vma=False,
    )
```

profile of v0, /device:TPU:0, one launch (start us, length us, event | category | flops | bytes accessed | tf_op | source)
XLA Modules:
  0.0 514.8 jit_solution(3046373207960037418)
XLA Ops:
  9.9 15.8 %all_gather.3 = bf16[16,256,32]{1,2,0:T(8,128)(2,1)S(1)} all-gather(bf16[4,256,32]{1,2,0:T(8,128)(2,1)} %param.15), channel_id=1, replica_groups=mesh['kp'=8,'ka'=4] {'ka'}, dimensions={0}, use_global_device_ids=true | all-gather | bytes 327680 | tf_op jit(solution)/shard_map/all_gather | solution.py:77
  27.2 3.7 all-to-all-start
  36.0 95.2 %all-reduce.12.cloned.1.call-done = (bf16[4,24,2048]{1,2,0:T(8,128)(2,1)}, bf16[4,128,128]{2,1,0:T(8,128)(2,1)}, bf16[512,64]{0,1:T(8,128)(2,1)}) async-done(((bf16[4,24,2048]{1,2,0:T(8,128)(2,1)}, bf16[4,128,128]{2,1,0:T(8,128)(2,1)}, bf16[512,64]{0,1:T(8,128)(2,1)}), (bf16[4,24,2048]{1,2,0:T(8,128)(2,1)}, bf16[4,128,128]{2,1,0:T(8,128)(2,1)}, bf16[512,64]{0,1:T(8,128)(2,1)})) %all-reduce.12.cloned.1.call-update) | async-done | bytes 589840 | tf_op jit(solution)/shard_map/psum | solution.py:14
  133.3 3.3 copy.69
  136.6 162.4 %while.10 = (s32[]{:T(128)}, bf16[8,128,128]{2,1,0:T(8,128)(2,1)S(1)}, s32[8]{0:T(128)S(1)}, bf16[4,128,128]{2,1,0:T(8,128)(2,1)}, bf16[4,24,2048]{2,1,0:T(8,128...) while((s32[]{:T(128)}, ...), condition=%wide.region_3.4_spmd, body=%wide.region_2.3_spmd.sunk | while | flops 125931528 | bytes 6739799 | solution.py:101
  142.6 6.2 %gather_fusion = bf16[2048,24]{1,0:T(8,128)(2,1)S(1)} fusion(bf16[24,2048]{0,1:T(8,128)(2,1)S(1)} %dynamic-slice_bitcast_fusion.4, s32[2048]{0:T(1024)S(1)} %broadcast_clamp_fusion.2), kind=kCustom, calls=%fused_computation.clone.1 | custom fusion | bytes 204800 | tf_op jit(solution)/shard_map/while/body/eval_jaxpr/jit(_take)/gather | solution.py:91
  152.3 1.5 fusion.106
  162.9 6.2 %gather_fusion = bf16[2048,24]{1,0:T(8,128)(2,1)S(1)} fusion(bf16[24,2048]{0,1:T(8,128)(2,1)S(1)} %dynamic-slice_bitcast_fusion.4, s32[2048]{0:T(1024)S(1)} %broadcast_clamp_fusion.2), kind=kCustom, calls=%fused_computation.clone.1 | custom fusion | bytes 204800 | tf_op jit(solution)/shard_map/while/body/eval_jaxpr/jit(_take)/gather | solution.py:91
  172.6 1.5 fusion.106
  183.2 6.2 %gather_fusion = bf16[2048,24]{1,0:T(8,128)(2,1)S(1)} fusion(bf16[24,2048]{0,1:T(8,128)(2,1)S(1)} %dynamic-slice_bitcast_fusion.4, s32[2048]{0:T(1024)S(1)} %broadcast_clamp_fusion.2), kind=kCustom, calls=%fused_computation.clone.1 | custom fusion | bytes 204800 | tf_op jit(solution)/shard_map/while/body/eval_jaxpr/jit(_take)/gather | solution.py:91
  192.9 1.5 fusion.106
  203.5 6.2 %gather_fusion = bf16[2048,24]{1,0:T(8,128)(2,1)S(1)} fusion(bf16[24,2048]{0,1:T(8,128)(2,1)S(1)} %dynamic-slice_bitcast_fusion.4, s32[2048]{0:T(1024)S(1)} %broadcast_clamp_fusion.2), kind=kCustom, calls=%fused_computation.clone.1 | custom fusion | bytes 204800 | tf_op jit(solution)/shard_map/while/body/eval_jaxpr/jit(_take)/gather | solution.py:91
  213.2 1.5 fusion.106
  223.8 6.2 %gather_fusion = bf16[2048,24]{1,0:T(8,128)(2,1)S(1)} fusion(bf16[24,2048]{0,1:T(8,128)(2,1)S(1)} %dynamic-slice_bitcast_fusion.4, s32[2048]{0:T(1024)S(1)} %broadcast_clamp_fusion.2), kind=kCustom, calls=%fused_computation.clone.1 | custom fusion | bytes 204800 | tf_op jit(solution)/shard_map/while/body/eval_jaxpr/jit(_take)/gather | solution.py:91
  233.5 1.5 fusion.106
  244.1 6.2 %gather_fusion = bf16[2048,24]{1,0:T(8,128)(2,1)S(1)} fusion(bf16[24,2048]{0,1:T(8,128)(2,1)S(1)} %dynamic-slice_bitcast_fusion.4, s32[2048]{0:T(1024)S(1)} %broadcast_clamp_fusion.2), kind=kCustom, calls=%fused_computation.clone.1 | custom fusion | bytes 204800 | tf_op jit(solution)/shard_map/while/body/eval_jaxpr/jit(_take)/gather | solution.py:91
  253.8 1.5 fusion.106
  264.4 6.2 %gather_fusion = bf16[2048,24]{1,0:T(8,128)(2,1)S(1)} fusion(bf16[24,2048]{0,1:T(8,128)(2,1)S(1)} %dynamic-slice_bitcast_fusion.4, s32[2048]{0:T(1024)S(1)} %broadcast_clamp_fusion.2), kind=kCustom, calls=%fused_computation.clone.1 | custom fusion | bytes 204800 | tf_op jit(solution)/shard_map/while/body/eval_jaxpr/jit(_take)/gather | solution.py:91
  274.1 1.5 fusion.106
  284.7 6.2 %gather_fusion = bf16[2048,24]{1,0:T(8,128)(2,1)S(1)} fusion(bf16[24,2048]{0,1:T(8,128)(2,1)S(1)} %dynamic-slice_bitcast_fusion.4, s32[2048]{0:T(1024)S(1)} %broadcast_clamp_fusion.2), kind=kCustom, calls=%fused_computation.clone.1 | custom fusion | bytes 204800 | tf_op jit(solution)/shard_map/while/body/eval_jaxpr/jit(_take)/gather | solution.py:91
  294.4 1.5 fusion.106
  300.3 52.1 %all-reduce.6.cloned.1.call-done = f32[512,64]{0,1:T(8,128)} async-done(((f32[512,64]{0,1:T(8,128)}), f32[512,64]{0,1:T(8,128)}) %all-reduce.6.cloned.1.call-update) | async-done | bytes 131088 | tf_op jit(solution)/shard_map/psum | solution.py:114
  353.6 19.0 %psum.60 = f32[64,64]{0,1:T(8,128)S(1)} all-reduce(f32[64,64]{0,1:T(8,128)S(1)} %fusion.36), channel_id=1, replica_groups=mesh['kp'=8,'ka'=4] {'ka'}, use_global_device_ids=true, to_apply=%region_6.7 | all-reduce | flops 4096 | bytes 32768 | tf_op jit(solution)/shard_map/psum | solution.py:118
  372.7 5.8 %cholesky.44 = f32[64,64]{1,0:T(8,128)S(1)} custom-call(f32[64,64]{1,0:T(8,128)S(1)} %fusion.43), custom_call_target="Cholesky" | custom-call | tf_op jit(solution)/shard_map/jit(cholesky)/cholesky | solution.py:119
  379.9 4.9 custom-call.6
  386.8 30.7 %all-reduce.8.cloned.1.call-done = bf16[512,64]{0,1:T(8,128)(2,1)} async-done(((bf16[512,64]{0,1:T(8,128)(2,1)}), bf16[512,64]{0,1:T(8,128)(2,1)}) %all-reduce.8.cloned.1.call-update) | async-done | bytes 65552 | tf_op jit(solution)/shard_map/psum | solution.py:14
  417.5 1.6 fusion.46
  419.2 54.8 %all-reduce.10.cloned.1.call-done = f32[512,64]{0,1:T(8,128)} async-done(((f32[512,64]{0,1:T(8,128)}), f32[512,64]{0,1:T(8,128)}) %all-reduce.10.cloned.1.call-update) | async-done | bytes 131088 | tf_op jit(solution)/shard_map/psum | solution.py:114
  475.2 19.0 %psum.63 = f32[64,64]{0,1:T(8,128)S(1)} all-reduce(f32[64,64]{0,1:T(8,128)S(1)} %fusion.37), channel_id=1, replica_groups=mesh['kp'=8,'ka'=4] {'ka'}, use_global_device_ids=true, to_apply=%region_11.14 | all-reduce | flops 4096 | bytes 32768 | tf_op jit(solution)/shard_map/psum | solution.py:118
  494.3 5.8 %cholesky.55 = f32[64,64]{1,0:T(8,128)S(1)} custom-call(f32[64,64]{1,0:T(8,128)S(1)} %fusion.41), custom_call_target="Cholesky" | custom-call | tf_op jit(solution)/shard_map/jit(cholesky)/cholesky | solution.py:119
  501.5 4.9 custom-call.7
  506.4 1.9 convolution_bitcast_fusion
  (256 shorter events, 73.2 us)
Async XLA Ops:
  7.2 0.7 copy-start
  8.8 22.2 %copy-start.2 = (bf16[4,24,2048]{2,1,0:T(8,128)(2,1)S(1)}, bf16[4,24,2048]{2,1,0:T(8,128)(2,1)}, u32[]{:S(2)}) copy-start(bf16[4,24,2048]{2,1,0:T(8,128)(2,1)} %param.13) | copy-start | bytes 1179652
  27.2 106.1 %all-to-all-start = ((bf16[8,8,256,32]{2,1,3,0:T(8,128)(2,1)}), bf16[8,8,256,32]{2,1,3,0:T(8,128)(2,1)S(1)}, u32[]{:S(2)}, u32[]{:S(2)}) async-start(bf16[8,8,256,32]{2,1,3,0:T(8,128)(2,1)} %convolution_convert_fusion.2), calls=%async_computation | async-start | bytes 2097152 | tf_op jit(solution)/shard_map/all_to_all | solution.py:84
  30.9 100.2 %all-reduce.12.cloned.1.call-start = ((), (), s32[]{:S(2)}) async-start(), calls=%async_computation.4 | async-start | bytes 4587520 | tf_op jit(solution)/shard_map/psum | solution.py:14
  32.1 1.5 copy-start.5
  32.1 2.1 copy-start.3
  34.9 317.5 %all-reduce.6.cloned.1.call-start = ((), (), s32[]{:S(2)}) async-start(), calls=%async_computation.1 | async-start | bytes 262144 | tf_op jit(solution)/shard_map/psum | solution.py:114
  133.3 3.3 copy-start.6
  136.6 162.8 %copy-start.8 = (bf16[512,64]{0,1:T(8,128)(2,1)S(1)}, bf16[512,64]{0,1:T(8,128)(2,1)}, u32[]{:S(2)}) copy-start(bf16[512,64]{0,1:T(8,128)(2,1)} %get-tuple-element.129) | copy-start | bytes 196612
  136.6 215.8 %copy-start.4 = (f32[512,64]{0,1:T(8,128)S(1)}, f32[512,64]{0,1:T(8,128)}, u32[]{:S(2)}) copy-start(f32[512,64]{0,1:T(8,128)} %param.20) | copy-start | bytes 393220
  136.6 215.8 %copy-start.7 = (f32[512]{0:T(512)S(1)}, f32[512]{0:T(512)}, u32[]{:S(2)}) copy-start(f32[512]{0:T(512)} %param.19) | copy-start | bytes 6148
  299.4 208.9 %copy-start.1 = (bf16[64,8,2,128]{3,1,2,0:T(8,128)(2,1)}, bf16[64,8,2,128]{3,1,2,0:T(8,128)(2,1)S(1)}, u32[]{:S(2)}) copy-start(bf16[64,8,2,128]{3,1,2,0:T(8,128)(2,1)S(1)} %copy.79) | copy-start | bytes 786436
  300.3 117.2 %all-reduce.8.cloned.1.call-start = ((), (), s32[]{:S(2)}) async-start(), calls=%async_computation.2 | async-start | bytes 131072 | tf_op jit(solution)/shard_map/psum | solution.py:14
  386.7 87.2 %all-reduce.10.cloned.1.call-start = ((), (), s32[]{:S(2)}) async-start(), calls=%async_computation.3 | async-start | bytes 262144 | tf_op jit(solution)/shard_map/psum | solution.py:114
Sparse Core Ops, SparseCore 0:
  35.0 96.1 all-reduce.11
  300.4 51.9 all-reduce.5
  386.9 30.5 all-reduce.7
  421.3 52.6 all-reduce.9
where the time goes:
time: 518 us; the launch traced here: 515 us
  waiting for transfers between devices  233 us (45%)
  local copies, waits for them, and re-layouts  79.7 us (15%)
  blocking collectives  53.8 us (10%)
  loops' own time  47.7 us (9%)
  matrix products  46.2 us (9%)
  other arithmetic  36.6 us (7%)
  between operations  14.1 us (3%)
    psum x2, waiting for transfers between devices, broadcast(): return lax.psum(block, axis)  126 us
    psum x2, waiting for transfers between devices, on_device(): images = energies[:, None] * vectors + lax.psum(product, 'kp')  107 us
    gather x16, local copies, waits for them, and re-layouts, one_pair(): mapped = jnp.take(far_form[far_slot], mapping, axis=1)  51 us
    another operation x1, loops' own time, on_device(): blocks = lax.map(one_pair, (near_slots, far_slots, transfers, pair_screen))  47.7 us
    psum x2, blocking collectives, on_device(): correlation = lax.psum(local_correlation, 'ka') / (total_points * pairs)  38 us
    all_gather x1, blocking collectives, on_device(): shard_piece = lax.all_gather(screen, 'ka', axis=0, tiled=True)  15.8 us
    dynamic_slice x24, local copies, waits for them, and re-layouts, on_device(): blocks = lax.map(one_pair, (near_slots, far_slots, transfers, pair_screen))  14.1 us
    another operation x6, other arithmetic, on_device(): factor = jnp.linalg.cholesky(correlation)  13 us
  transfers between devices with their start and end apart: 5, of which 4 were waited for; matrix products, arithmetic and copies ran while one was open for 1% of the time, Pallas kernels for 0%

commit v1 on v0

v1 whole, which is shorter than its diff:
```python
import functools

import jax
import jax.numpy as jnp
from jax import lax
from jax.experimental import pallas as pl
from jax.experimental.pallas import tpu as pltpu
from jax.sharding import PartitionSpec as P

NV = 8
NC = 16
STEPS = 2
GRID_Y = 8
LANES = 128
CHUNK = 512
MESH = pl.DeviceIdType.MESH
VMEM = pl.BlockSpec(memory_space=pltpu.VMEM)
SMEM = pl.BlockSpec(memory_space=pltpu.SMEM)
NT = (((1,), (1,)), ((), ()))
F32 = jnp.float32
BF16 = jnp.bfloat16


def exchange_kernel(
    size_ka, size_kp, form, coef, start, cols,
    far_form, far_coef, far_start, all_cols,
    up_sem, down_sem, far_sem,
    z_send, z_recv, plane_send, plane_recv, core_send, core_recv,
):
    ka, kp = lax.axis_index("ka"), lax.axis_index("kp")
    chips = size_kp // 2
    chip, core = kp // 2, kp % 2
    near, far = form.shape[0], far_form.shape[0]
    rows = cols.shape[0]
    owner = kp * far // near
    offset = kp * far % near

    barrier = pltpu.get_barrier_semaphore()

    def greet_z(d, carry):
        pl.semaphore_signal(barrier, inc=1, device_id={"ka": (ka + d) % size_ka}, device_id_type=MESH)
        return carry

    def greet_plane(d, carry):
        other = (chip + d) % chips * 2 + core
        pl.semaphore_signal(barrier, inc=1, device_id={"kp": other}, device_id_type=MESH)
        return carry

    lax.fori_loop(1, size_ka, greet_z, 0)
    lax.fori_loop(1, chips, greet_plane, 0)
    pl.semaphore_signal(barrier, inc=1, device_id={"kp": chip * 2 + 1 - core}, device_id_type=MESH)
    pl.semaphore_wait(barrier, size_ka - 1 + chips - 1 + 1)

    pieces = [far_form.at[i] for i in range(far)] + [far_coef, far_start]

    def far_copy(i, sem, target):
        return pltpu.make_async_remote_copy(
            src_ref=pieces[i], dst_ref=pieces[i], send_sem=sem.at[i], recv_sem=far_sem.at[i],
            device_id={"ka": target}, device_id_type=MESH,
        )

    goes_up = (ka >= owner) & (ka < size_ka - 1)
    goes_down = (ka <= owner) & (ka > 0)
    above, below = lax.rem(ka + 1, size_ka), lax.rem(ka + size_ka - 1, size_ka)

    def part(z, p):
        return all_cols.at[z, pl.ds(pl.multiple_of(p * rows, rows), rows), :]

    def z_copy(z, target):
        return pltpu.make_async_remote_copy(
            src_ref=part(z, kp), dst_ref=part(z, kp), send_sem=z_send.at[target],
            recv_sem=z_recv.at[z], device_id={"ka": target}, device_id_type=MESH,
        )

    def plane_copy(z, source, target):
        ref = part(z, source * 2 + core)
        return pltpu.make_async_remote_copy(
            src_ref=ref, dst_ref=ref, send_sem=plane_send.at[z, target],
            recv_sem=plane_recv.at[z, source],
            device_id={"kp": target * 2 + core}, device_id_type=MESH,
        )

    def core_copy(z, c, from_core):
        ref = part(z, c * 2 + from_core)
        return pltpu.make_async_remote_copy(
            src_ref=ref, dst_ref=ref, send_sem=core_send.at[z, c], recv_sem=core_recv.at[z, c],
            device_id={"kp": chip * 2 + 1 - core}, device_id_type=MESH,
        )

    @pl.when(ka == owner)
    def _():
        far_form[...] = form[pl.ds(offset, far)]
        far_coef[...] = coef[pl.ds(offset, far)]
        far_start[...] = start[pl.ds(offset, far)]

    all_cols[ka, pl.ds(pl.multiple_of(kp * rows, rows), rows), :] = cols[...]

    def spread(z):
        def to_plane(d, carry):
            plane_copy(z, chip, (chip + d) % chips).start()
            return carry

        lax.fori_loop(1, chips, to_plane, 0)
        core_copy(z, chip, core).start()

    def forward(i):
        @pl.when(goes_up)
        def _():
            far_copy(i, up_sem, above).start()

        @pl.when(goes_down)
        def _():
            far_copy(i, down_sem, below).start()

    @pl.when(ka == owner)
    def _():
        for i in range(len(pieces)):
            forward(i)

    def to_z(d, carry):
        z_copy(ka, (ka + d) % size_ka).start()
        return carry

    lax.fori_loop(1, size_ka, to_z, 0)
    spread(ka)

    @pl.when(ka != owner)
    def _():
        for i in range(len(pieces)):
            far_copy(i, up_sem, above).wait_recv()
            forward(i)

    def from_z(d, carry):
        z = (ka + size_ka - d) % size_ka
        z_copy(z, above).wait_recv()
        spread(z)
        return carry

    lax.fori_loop(1, size_ka, from_z, 0)

    def from_plane(d, carry):
        z = (ka + size_ka - d) % size_ka

        def one(e, inner):
            c = (chip + chips - e) % chips
            plane_copy(z, c, (chip + e) % chips).wait_recv()
            core_copy(z, c, core).start()
            return inner

        return lax.fori_loop(1, chips, one, carry)

    lax.fori_loop(0, size_ka, from_plane, 0)

    def finish(n, carry):
        z, c = n // chips, n % chips
        core_copy(z, c, 1 - core).wait_recv()
        core_copy(z, c, core).wait_send()
        return carry

    lax.fori_loop(0, size_ka * chips, finish, 0)

    def finish_plane(n, carry):
        z, e = n // (chips - 1), n % (chips - 1) + 1
        plane_copy(z, chip, (chip + e) % chips).wait_send()
        return carry

    lax.fori_loop(0, size_ka * (chips - 1), finish_plane, 0)

    def finish_z(d, carry):
        z_copy(ka, (ka + d) % size_ka).wait_send()
        return carry

    lax.fori_loop(1, size_ka, finish_z, 0)
    for i in range(len(pieces)):
        @pl.when(goes_up)
        def _():
            far_copy(i, up_sem, above).wait_send()

        @pl.when(goes_down)
        def _():
            far_copy(i, down_sem, below).wait_send()


def exchange(size_ka, size_kp, far, form, coef, start, cols):
    chips = size_kp // 2
    pieces = far + 2
    dma = pltpu.SemaphoreType.DMA
    return pl.pallas_call(
        functools.partial(exchange_kernel, size_ka, size_kp),
        out_shape=(
            jax.ShapeDtypeStruct((far,) + form.shape[1:], BF16),
            jax.ShapeDtypeStruct((far,) + coef.shape[1:], BF16),
            jax.ShapeDtypeStruct((far,) + start.shape[1:], BF16),
            jax.ShapeDtypeStruct((size_ka, cols.shape[0] * size_kp, cols.shape[1]), BF16),
        ),
        in_specs=[VMEM] * 4,
        out_specs=(VMEM,) * 4,
        scratch_shapes=[
            dma((pieces,)), dma((pieces,)), dma((pieces,)),
            dma((size_ka,)), dma((size_ka,)),
            dma((size_ka, chips)), dma((size_ka, chips)),
            dma((size_ka, chips)), dma((size_ka, chips)),
        ],
        compiler_params=pltpu.CompilerParams(
            collective_id=0, has_side_effects=True, vmem_limit_bytes=48 * 2**20
        ),
    )(form, coef, start, cols)


def blocks_kernel(
    near, far, group, transfers, form, far_form, coef_t, far_coef, all_cols, coulomb, shift_map,
    out, flat, direct, packed,
):
    waves = form.shape[2]
    pieces = waves // LANES
    bands = NV + NC
    per_owner = all_cols.shape[2] // group
    flat[...] = jnp.zeros_like(flat)
    for f in range(far):
        for h in range(pieces):
            flat[f, h, 0:bands, :] = far_form[f, :, h * LANES : (h + 1) * LANES]

    def one_pair(n, carry):
        k, f = n // far, n % far
        q = transfers[n]
        source = flat[f].reshape(pieces * flat.shape[2], LANES)
        height = flat.shape[2]
        owner = q // per_owner
        total = jnp.zeros((NV * NV, NC * NC), F32)
        left = jnp.zeros((NC * NC, all_cols.shape[2]), F32)
        right = jnp.zeros((NV * NV, all_cols.shape[2]), F32)
        for s in range(0, waves, CHUNK):
            index = shift_map[q, :, s : s + CHUNK]
            low = index & (LANES - 1)
            high = index >> 7
            one_hot = jnp.where(
                lax.broadcasted_iota(jnp.int32, (LANES, CHUNK), 0) == low, 1.0, 0.0
            ).astype(BF16)
            spread = jnp.dot(source, one_hot, preferred_element_type=F32)
            mapped = spread[0:bands]
            for h in range(1, pieces):
                mapped = jnp.where(high == h, spread[h * height : h * height + bands], mapped)
            near_form = form[k, :, s : s + CHUNK].astype(F32)
            valence = jnp.concatenate(
                [near_form[v : v + 1] * mapped[0:NV] for v in range(NV)], axis=0
            ).astype(BF16)
            conduction = jnp.concatenate(
                [near_form[NV + c : NV + c + 1] * mapped[NV:] for c in range(NC)], axis=0
            ).astype(BF16)
            scaled = (coulomb[:, s : s + CHUNK] * valence.astype(F32)).astype(BF16)
            columns = all_cols[owner, s : s + CHUNK, :]
            total += lax.dot_general(scaled, conduction, NT, preferred_element_type=F32)
            left += jnp.dot(conduction, columns, preferred_element_type=F32)
            right += jnp.dot(valence, columns, preferred_element_type=F32)
        lane = lax.broadcasted_iota(jnp.int32, right.shape, 1)
        right = jnp.where(lane // group == q % per_owner, right, 0.0)
        total += lax.dot_general(
            right, left, NT, precision=lax.Precision.HIGHEST, preferred_element_type=F32
        )
        rows = NV * NV
        direct[pl.ds(pl.multiple_of(n * rows, rows), rows), :] = total.astype(BF16)
        return carry

    pairs = near * far
    lax.fori_loop(0, pairs, one_pair, 0)

    all_rows = pairs * NV * NV
    row = lax.broadcasted_iota(jnp.int32, (all_rows, LANES), 0)
    lane = lax.broadcasted_iota(jnp.int32, (all_rows, LANES), 1)
    keep = row % NV == lane // NC
    sum_row = lax.broadcasted_iota(jnp.int32, (pairs * NV, all_rows), 0)
    sum_col = lax.broadcasted_iota(jnp.int32, (pairs * NV, all_rows), 1)
    sums = jnp.where(sum_col // NV == sum_row, 1.0, 0.0).astype(BF16)
    pick_row = lax.broadcasted_iota(jnp.int32, (LANES, LANES), 0)
    pick_lane = lax.broadcasted_iota(jnp.int32, (LANES, LANES), 1)
    per_half = LANES // NC
    for c in range(NC):
        pick = jnp.where(
            (pick_row // NC == c % per_half) & (pick_row % NC == pick_lane % NC), 1.0, 0.0
        ).astype(BF16)
        half_at = c // per_half * LANES
        wide = jnp.dot(direct[:, half_at : half_at + LANES], pick, preferred_element_type=F32)
        wide = jnp.where(keep, wide, 0.0).astype(BF16)
        rows = jnp.dot(sums, wide, preferred_element_type=F32)
        packed[:, c * NV : (c + 1) * NV, :] = rows.reshape(pairs, NV, LANES)
    side = NV * NC
    for k in range(near):
        for f in range(far):
            block = packed[k * far + f].astype(BF16)
            half = jnp.dot(block, far_coef[f], preferred_element_type=F32).astype(BF16)
            out[k * side : (k + 1) * side, f * side : (f + 1) * side] = jnp.dot(
                coef_t[k], half, preferred_element_type=F32
            ).astype(BF16)


def blocks(near, far, group, transfers, form, far_form, coef_t, far_coef, all_cols, coulomb, shift_map):
    waves = form.shape[2]
    side = NV * NC
    pairs = near * far
    return pl.pallas_call(
        functools.partial(blocks_kernel, near, far, group),
        out_shape=jax.ShapeDtypeStruct((near * side, far * side), BF16),
        in_specs=[SMEM] + [VMEM] * 7,
        out_specs=VMEM,
        scratch_shapes=[
            pltpu.VMEM((far, waves // LANES, 32, LANES), BF16),
            pltpu.VMEM((pairs * NV * NV, NC * NC), BF16),
            pltpu.VMEM((pairs, side, LANES), F32),
        ],
        compiler_params=pltpu.CompilerParams(vmem_limit_bytes=48 * 2**20),
    )(transfers, form, far_form, coef_t, far_coef, all_cols, coulomb, shift_map)


def inverse_factor(matrix):
    size = matrix.shape[0]
    row = lax.broadcasted_iota(jnp.int32, matrix.shape, 0)
    lane = lax.broadcasted_iota(jnp.int32, matrix.shape, 1)
    work = jnp.where(lane == row + size, 1.0, matrix)
    for j in range(size - 1):
        pivot_row = work[j : j + 1, :]
        scaled_row = pivot_row / pivot_row[:, j : j + 1]
        work = work - jnp.where(row > j, work[:, j : j + 1], 0.0) * scaled_row
    diagonal = jnp.sum(jnp.where(lane == row, work, 0.0), axis=1, keepdims=True)
    return jnp.where(lane >= size, work * lax.rsqrt(diagonal), 0.0)


def subspace_kernel(
    size_ka, size_kp, kernel, far_start, energies, start, out,
    product, image, far_image, far_bf16, received, correlations,
    rs_send, rs_recv, ag_send, ag_recv, z_send, z_recv, far_send, far_recv,
):
    ka, kp = lax.axis_index("ka"), lax.axis_index("kp")
    vectors, rows = start.shape
    far, _, side = far_start.shape
    near = rows // side
    owner = kp * far // near
    offset = kp * far % near
    row_groups = vectors // 8
    lane_groups = size_kp // row_groups
    width = rows // lane_groups
    total_rows = rows * size_ka

    barrier = pltpu.get_barrier_semaphore()

    def greet_z(d, carry):
        pl.semaphore_signal(barrier, inc=1, device_id={"ka": (ka + d) % size_ka}, device_id_type=MESH)
        return carry

    def greet_plane(d, carry):
        pl.semaphore_signal(barrier, inc=1, device_id={"kp": (kp + d) % size_kp}, device_id_type=MESH)
        return carry

    lax.fori_loop(1, size_ka, greet_z, 0)
    lax.fori_loop(1, size_kp, greet_plane, 0)

    def chunk(p):
        return (
            pl.ds(pl.multiple_of(p // lane_groups * 8, 8), 8),
            pl.ds(pl.multiple_of(p % lane_groups * width, width), width),
        )

    own_rows, own_lanes = chunk(kp)
    padding = jnp.zeros((vectors, rows), F32)

    for step in range(STEPS):
        def rs_copy(source, target):
            return pltpu.make_async_remote_copy(
                src_ref=product.at[step].at[chunk(target)],
                dst_ref=received.at[step, source],
                send_sem=rs_send.at[step, target], recv_sem=rs_recv.at[step, source],
                device_id={"kp": target}, device_id_type=MESH,
            )

        def ag_copy(source, target):
            ref = image.at[step].at[chunk(source)]
            return pltpu.make_async_remote_copy(
                src_ref=ref, dst_ref=ref,
                send_sem=ag_send.at[step, target], recv_sem=ag_recv.at[step, source],
                device_id={"kp": target}, device_id_type=MESH,
            )

        def z_copy(source, target):
            ref = correlations.at[step, source]
            return pltpu.make_async_remote_copy(
                src_ref=ref, dst_ref=ref,
                send_sem=z_send.at[step, target], recv_sem=z_recv.at[step, source],
                device_id={"ka": target}, device_id_type=MESH,
            )

        def far_copy(target):
            return pltpu.make_async_remote_copy(
                src_ref=far_image.at[step], dst_ref=far_image.at[step],
                send_sem=far_send.at[step, target], recv_sem=far_recv.at[step],
                device_id={"ka": target}, device_id_type=MESH,
            )

        def loop(first, count, body):
            def one(d, carry):
                body(d)
                return carry

            lax.fori_loop(first, count, one, 0)

        total = jnp.zeros((vectors, rows), F32)
        for f in range(far):
            far_vectors = far_start[f] if step == 0 else far_bf16[f]
            total += lax.dot_general(
                far_vectors, kernel[:, f * side : (f + 1) * side], NT, preferred_element_type=F32
            )
        product[step] = total
        if step == 0:
            pl.semaphore_wait(barrier, size_ka - 1 + size_kp - 1)
        loop(1, size_kp, lambda d: rs_copy(kp, (kp + d) % size_kp).start())
        received[step, kp] = product[step, own_rows, own_lanes]
        loop(1, size_kp, lambda d: rs_copy((kp + size_kp - d) % size_kp, kp).wait_recv())
        current = start if step == 0 else out
        value = energies[:, own_lanes] * current[own_rows, own_lanes]
        image[step, own_rows, own_lanes] = value + jnp.sum(received[step], axis=0)
        loop(1, size_kp, lambda d: ag_copy(kp, (kp + d) % size_kp).start())
        loop(1, size_kp, lambda d: ag_copy((kp + size_kp - d) % size_kp, kp).wait_recv())
        whole = image[step]
        correlations[step, ka] = lax.dot_general(
            whole, jnp.concatenate([whole, padding], axis=0), NT,
            precision=lax.Precision.HIGHEST, preferred_element_type=F32,
        )
        loop(1, size_ka, lambda d: z_copy(ka, (ka + d) % size_ka).start())
        if step + 1 < STEPS:
            @pl.when(ka == owner)
            def _():
                for f in range(far):
                    far_image[step, f] = image[
                        step, :, pl.ds(pl.multiple_of((offset + f) * side, side), side)
                    ].astype(BF16)
                loop(1, size_ka, lambda d: far_copy((ka + d) % size_ka).start())
        loop(1, size_ka, lambda d: z_copy((ka + size_ka - d) % size_ka, ka).wait_recv())
        correlation = correlations[step, 0]
        for z in range(1, size_ka):
            correlation = correlation + correlations[step, z]
        inverse = inverse_factor(correlation * (1.0 / total_rows))
        out[...] = jnp.dot(
            inverse, jnp.concatenate([padding, whole], axis=0),
            precision=lax.Precision.HIGHEST, preferred_element_type=F32,
        )
        if step + 1 < STEPS:
            @pl.when(ka != owner)
            def _():
                far_copy(ka).wait_recv()

            for f in range(far):
                far_bf16[f] = jnp.dot(
                    inverse,
                    jnp.concatenate([padding[:, :side], far_image[step, f].astype(F32)], axis=0),
                    precision=lax.Precision.HIGHEST, preferred_element_type=F32,
                ).astype(BF16)

            @pl.when(ka == owner)
            def _():
                loop(1, size_ka, lambda d: far_copy((ka + d) % size_ka).wait_send())
        loop(1, size_kp, lambda d: rs_copy(kp, (kp + d) % size_kp).wait_send())
        loop(1, size_kp, lambda d: ag_copy(kp, (kp + d) % size_kp).wait_send())
        loop(1, size_ka, lambda d: z_copy(ka, (ka + d) % size_ka).wait_send())


def subspace(size_ka, size_kp, kernel, far_start, energies, start):
    vectors, rows = start.shape
    far, _, side = far_start.shape
    width = rows // (size_kp // (vectors // 8))
    dma = pltpu.SemaphoreType.DMA
    return pl.pallas_call(
        functools.partial(subspace_kernel, size_ka, size_kp),
        out_shape=jax.ShapeDtypeStruct((vectors, rows), F32),
        in_specs=[VMEM] * 4,
        out_specs=VMEM,
        scratch_shapes=[
            pltpu.VMEM((STEPS, vectors, rows), F32),
            pltpu.VMEM((STEPS, vectors, rows), F32),
            pltpu.VMEM((STEPS, far, vectors, side), BF16),
            pltpu.VMEM((far, vectors, side), BF16),
            pltpu.VMEM((STEPS, size_kp, 8, width), F32),
            pltpu.VMEM((STEPS, size_ka, vectors, 2 * vectors), F32),
            dma((STEPS, size_kp)), dma((STEPS, size_kp)),
            dma((STEPS, size_kp)), dma((STEPS, size_kp)),
            dma((STEPS, size_ka)), dma((STEPS, size_ka)),
            dma((STEPS, size_ka)), dma((STEPS,)),
        ],
        compiler_params=pltpu.CompilerParams(
            collective_id=1, has_side_effects=True, vmem_limit_bytes=32 * 2**20
        ),
    )(kernel, far_start, energies, start)


def transfer_table(near_cells, far_cells, grid_x):
    step_x = (near_cells[:, None] // GRID_Y - far_cells[None, :] // GRID_Y) % grid_x
    step_y = (near_cells[:, None] % GRID_Y - far_cells[None, :] % GRID_Y) % GRID_Y
    return (step_x * GRID_Y + step_y).reshape(-1)


def on_device(band_form, interp_coef, screen, coulomb, shift_map, grid_order, energies, initial):
    size_ka = lax.axis_size("ka")
    size_kp = lax.axis_size("kp")
    near = band_form.shape[0]
    points = near * size_ka
    far = points // size_kp
    side = interp_coef.shape[1]
    near_cells = lax.dynamic_slice_in_dim(grid_order, lax.axis_index("ka") * near, near)
    far_cells = lax.dynamic_slice_in_dim(grid_order, lax.axis_index("kp") * far, far)
    transfers = transfer_table(near_cells, far_cells, points // GRID_Y)
    start = initial.T
    start_points = initial.astype(BF16).reshape(near, side, -1).transpose(0, 2, 1)
    cols = screen.transpose(1, 0, 2).reshape(screen.shape[1], -1)
    coef_t = interp_coef.reshape(near, NV, NC, side).transpose(0, 3, 2, 1).reshape(near, side, side)
    far_form, far_coef, far_start, all_cols = exchange(
        size_ka, size_kp, far, band_form, interp_coef, start_points, cols
    )
    kernel = blocks(
        near, far, screen.shape[2], transfers, band_form, far_form, coef_t, far_coef, all_cols,
        coulomb[None, :], shift_map[:, None, :],
    )
    out = subspace(size_ka, size_kp, kernel, far_start, energies[None, :], start)
    return kernel, out.T


def solution(mesh):
    return jax.shard_map(
        on_device,
        mesh=mesh,
        in_specs=(
            P("ka", None, None),
            P("ka", None, None),
            P("ka", "kp", None),
            P(),
            P(),
            P(),
            P("ka"),
            P("ka", None),
        ),
        out_specs=(P("ka", "kp"), P("ka", None)),
        check_vma=False,
    )
```

time: 518 us -> 107 us (0.21)
  waiting for transfers between devices: 233 us -> 0 us
  Pallas kernels: 0 us -> 94.7 us
  local copies, waits for them, and re-layouts: 79.7 us -> 7.4 us
  blocking collectives: 53.8 us -> 0 us
  loops' own time: 47.7 us -> 0 us
  matrix products: 46.2 us -> 0 us
  other arithmetic: 36.6 us -> 4.02 us
  between operations: 14.1 us -> 0.71 us
    psum x4 -> x0, waiting for transfers between devices: 233 us -> none  [the longest x2 126 us: broadcast(): return lax.psum(block, axis)]
    pallas_call x0 -> x3, Pallas kernels: none -> 94.7 us  [the longest x1 38 us: subspace(): pl.pallas_call(functools.partial(subspace_kernel, size_ka, size_kp), out_...]
    gather x20 -> x0, local copies, waits for them, and re-layouts: 53 us -> none  [the longest x16 51 us: one_pair(): mapped = jnp.take(far_form[far_slot], mapping, axis=1)]
    another operation x1 -> x0, loops' own time: 47.7 us -> none  [on_device(): blocks = lax.map(one_pair, (near_slots, far_slots, transfers, pair_screen))]
    dot_general x45 -> x0, matrix products: 43.1 us -> none  [the longest x8 11.8 us: pair_block(): left = jnp.dot(conduction, screen_cols, preferred_element_type=jnp.float32)]
    psum x2 -> x0, blocking collectives: 38 us -> none  [on_device(): correlation = lax.psum(local_correlation, 'ka') / (total_points * pairs)]
    another operation x10 -> x0, other arithmetic: 24.2 us -> none  [the longest x6 13 us: on_device(): factor = jnp.linalg.cholesky(correlation)]
    dynamic_slice x26 -> x0, local copies, waits for them, and re-layouts: 16.3 us -> none  [the longest x24 14.1 us: on_device(): blocks = lax.map(one_pair, (near_slots, far_slots, transfers, pair_screen))]
  transfers between devices with their start and end apart: 5 -> 0, of which waited for: 4 -> 0; matrix products, arithmetic and copies ran while one was open for 1% -> 0% of each run, Pallas kernels for 0% -> 0%
where the time goes in v1:
time: 107 us
  Pallas kernels  94.7 us (89%)
  local copies, waits for them, and re-layouts  7.4 us (7%)
  other arithmetic  4.02 us (4%)
    pallas_call x1, Pallas kernels, subspace(): pl.pallas_call(functools.partial(subspace_kernel, size_ka, size_kp), out_...  38 us
    pallas_call x1, Pallas kernels, exchange(): pl.pallas_call(functools.partial(exchange_kernel, size_ka, size_kp), out_...  35.1 us
    pallas_call x1, Pallas kernels, blocks(): pl.pallas_call(functools.partial(blocks_kernel, near, far, group), out_sh...  21.6 us
    unnamed x13, local copies, waits for them, and re-layouts  4.21 us

profile of v1, /device:TPU:0, one launch (start us, length us, event | category | flops | bytes accessed | tf_op | source)
XLA Modules:
  0.0 106.8 jit_solution(13229813735964568415)
XLA Ops:
  0.6 0.7 and_select_fusion.2
  1.4 0.7 and_select_fusion.5
  2.1 0.7 and_select_fusion.1
  2.8 0.7 and_select_fusion.4
  3.6 0.1 broadcast_subtract_fusion.1
  3.7 0.1 sub.47
  3.7 0.1 broadcast_subtract_fusion
  3.8 0.1 sub.51
  3.9 1.0 copy.16.cols
  4.9 0.9 bitcast_bitcast_fusion.start
  5.8 1.0 broadcast_in_dim.14.shift_map
  6.8 0.9 copy.22
  7.7 0.0 copy-start.3
  7.7 0.0 copy-start.5
  7.8 0.1 copy.18.coef_t
  7.9 0.0 copy-start
  7.9 1.0 copy-done
  8.9 0.0 copy-start.2
  8.9 0.9 copy-done.2
  9.8 35.1 %shard_map.95 = (bf16[2,24,2048]{2,1,0:T(8,128)(2,1)S(1)}, bf16[2,128,128]{2,1,0:T(8,128)(2,1)S(1)}, bf16[2,64,128]{2,1,0:T(8,128)(2,1)S(1)}, bf16[4,2048,128]{2,1,0:T(8,128)(2,1)S(1)}) custom-call(bf16[4,24,2048]{2,1,0:T(8,128)(2,1)S(1)} %copy-done, bf16[4,128,128]{2,1,0:T(8,128)(2,1)S(1)} %copy-done.2, bf16[4,64,128]{2,1,0:T(8,128)(2,1)S(1)} %bitcast_bitcast_fusion.start, ...), custom_call_target="tpu_custom_call" | custom-call | tf_op jit(solution)/shard_map/pallas_call | solution.py:188
  44.9 0.0 copy-start.4
  44.9 0.7 copy-done.4
  45.6 21.6 %shard_map.96.kernel = bf16[512,256]{1,0:T(8,128)(2,1)} custom-call(s32[8]{0:T(128)S(1)} %fusion.transfers, bf16[4,24,2048]{2,1,0:T(8,128)(2,1)S(1)} %copy-done, bf16[2,24,2048]{2,1,0:T(8,128)(2,1)S(1)} %get-tuple-element.6.far_form, bf16[4,128,128]{2,1,0:T(8,128)(2,1)S(1)} %copy.18.coef_t, bf16[2,128,128]{2,1,0:T(8,128)(2,1)S(1)} %get-tuple-element.7.far_coef, ...), custom_call_target="tpu_custom_call" | custom-call | tf_op jit(solution)/shard_map/pallas_call | solution.py:300
  67.2 0.0 copy-done.3
  67.2 0.0 copy-done.5
  67.2 0.0 copy-start.1
  67.2 0.9 copy-done.1
  68.1 38.0 %shard_map.97 = f32[64,512]{1,0:T(8,128)S(1)} custom-call(bf16[512,256]{1,0:T(8,128)(2,1)S(1)} %copy-done.1, bf16[2,64,128]{2,1,0:T(8,128)(2,1)S(1)} %get-tuple-element.9.far_start, f32[1,512]{1,0:T(1,128)S(1)} %bitcast.24, f32[64,512]{1,0:T(8,128)S(1)} %bitcast.21), custom_call_target="tpu_custom_call" | custom-call | tf_op jit(solution)/shard_map/pallas_call | solution.py:469
  106.2 0.7 copy.24
  (1 shorter events, 0.0 us)
Async XLA Ops:
  7.7 59.4 %copy-start.3 = (f32[512,64]{0,1:T(8,128)S(1)}, f32[512,64]{0,1:T(8,128)}, u32[]{:S(2)}) copy-start(f32[512,64]{0,1:T(8,128)} %param.15) | copy-start | bytes 393220
  7.7 59.4 %copy-start.5 = (f32[512]{0:T(512)S(1)}, f32[512]{0:T(512)}, u32[]{:S(2)}) copy-start(f32[512]{0:T(512)} %param.14) | copy-start | bytes 6148
  7.9 1.0 copy-start
  8.9 0.9 copy-start.2
  44.9 0.7 copy-start.4
  67.2 1.0 copy-start.1

commit v2 on v0

v2 whole, which is shorter than its diff:
```python
import functools

import jax
import jax.numpy as jnp
from jax import lax
from jax.experimental import pallas as pl
from jax.experimental.pallas import tpu as pltpu
from jax.sharding import PartitionSpec as P

NV = 8
NC = 16
STEPS = 2
GRID_Y = 8
LANES = 128
CHUNK = 512
MESH = pl.DeviceIdType.MESH
VMEM = pl.BlockSpec(memory_space=pltpu.VMEM)
SMEM = pl.BlockSpec(memory_space=pltpu.SMEM)
NT = (((1,), (1,)), ((), ()))
TN = (((0,), (0,)), ((), ()))
F32 = jnp.float32
BF16 = jnp.bfloat16


def inverse_factor(matrix):
    size = matrix.shape[0]
    row = lax.broadcasted_iota(jnp.int32, matrix.shape, 0)
    lane = lax.broadcasted_iota(jnp.int32, matrix.shape, 1)
    work = jnp.where(lane == row + size, 1.0, matrix)
    for j in range(size - 1):
        pivot_row = work[j : j + 1, :]
        scaled_row = pivot_row / pivot_row[:, j : j + 1]
        work = work - jnp.where(row > j, work[:, j : j + 1], 0.0) * scaled_row
    diagonal = jnp.sum(jnp.where(lane == row, work, 0.0), axis=1, keepdims=True)
    return jnp.where(lane >= size, work * lax.rsqrt(diagonal), 0.0)


def whole_kernel(
    size_ka, size_kp,
    grid_order, form, coef, screen, coulomb, shift_map, energies, initial,
    kernel, subspace,
    far_form, far_coef, far_start, all_cols, source, conductions, valences, direct, packed, start,
    product, image, far_image, far_bf16, received, correlations,
    up_sem, down_sem, far_sem, z_send, z_recv, plane_send, plane_recv, core_send, core_recv,
    rs_send, rs_recv, ag_send, ag_recv, c_send, c_recv, far_send, far_recv,
):
    ka, kp = lax.axis_index("ka"), lax.axis_index("kp")
    chips = size_kp // 2
    chip, core = kp // 2, kp % 2
    near, far = form.shape[0], far_form.shape[0]
    owner = kp * far // near
    offset = kp * far % near
    per_owner, cut, group = screen.shape
    waves = form.shape[2]
    pieces = waves // LANES
    bands = NV + NC
    side = NV * NC
    pairs = near * far
    grid_x = near * size_ka // GRID_Y

    barrier = pltpu.get_barrier_semaphore()

    def greet_z(d, carry):
        pl.semaphore_signal(barrier, inc=1, device_id={"ka": (ka + d) % size_ka}, device_id_type=MESH)
        return carry

    def greet_plane(d, carry):
        pl.semaphore_signal(barrier, inc=1, device_id={"kp": (kp + d) % size_kp}, device_id_type=MESH)
        return carry

    lax.fori_loop(1, size_ka, greet_z, 0)
    lax.fori_loop(1, size_kp, greet_plane, 0)

    @pl.when(ka == owner)
    def _():
        far_form[...] = form[pl.ds(offset, far)]
        far_coef[...] = coef[pl.ds(offset, far)]
        for f in range(far):
            rows = pl.ds(pl.multiple_of((offset + f) * side, side), side)
            far_start[f] = initial[rows, :].T.astype(BF16)

    def part(z, p):
        return all_cols.at[z, pl.ds(pl.multiple_of(p * cut, cut), cut), :]

    all_cols[ka, pl.ds(pl.multiple_of(kp * cut, cut), cut), :] = jnp.concatenate(
        [screen[n] for n in range(per_owner)], axis=1
    )
    pl.semaphore_wait(barrier, size_ka - 1 + size_kp - 1)

    sent = [far_form.at[i] for i in range(far)] + [far_coef, far_start]

    def far_move(i, sem, target):
        return pltpu.make_async_remote_copy(
            src_ref=sent[i], dst_ref=sent[i], send_sem=sem.at[i], recv_sem=far_sem.at[i],
            device_id={"ka": target}, device_id_type=MESH,
        )

    goes_up = (ka >= owner) & (ka < size_ka - 1)
    goes_down = (ka <= owner) & (ka > 0)
    above, below = (ka + 1) % size_ka, (ka + size_ka - 1) % size_ka

    def z_move(z, target):
        return pltpu.make_async_remote_copy(
            src_ref=part(z, kp), dst_ref=part(z, kp), send_sem=z_send.at[target],
            recv_sem=z_recv.at[z], device_id={"ka": target}, device_id_type=MESH,
        )

    def plane_move(z, c, target):
        ref = part(z, c * 2 + core)
        return pltpu.make_async_remote_copy(
            src_ref=ref, dst_ref=ref, send_sem=plane_send.at[z, target],
            recv_sem=plane_recv.at[z, c],
            device_id={"kp": target * 2 + core}, device_id_type=MESH,
        )

    def core_move(z, c, from_core):
        ref = part(z, c * 2 + from_core)
        return pltpu.make_async_remote_copy(
            src_ref=ref, dst_ref=ref, send_sem=core_send.at[z, c], recv_sem=core_recv.at[z, c],
            device_id={"kp": chip * 2 + 1 - core}, device_id_type=MESH,
        )

    def spread(z):
        def to_plane(d, carry):
            plane_move(z, chip, (chip + d) % chips).start()
            return carry

        lax.fori_loop(1, chips, to_plane, 0)
        core_move(z, chip, core).start()

    def forward(i):
        @pl.when(goes_up)
        def _():
            far_move(i, up_sem, above).start()

        @pl.when(goes_down)
        def _():
            far_move(i, down_sem, below).start()

    @pl.when(ka == owner)
    def _():
        for i in range(len(sent)):
            forward(i)

    def to_z(d, carry):
        z_move(ka, (ka + d) % size_ka).start()
        return carry

    lax.fori_loop(1, size_ka, to_z, 0)
    spread(ka)

    def relay(first, last):
        @pl.when(ka != owner)
        def _():
            for i in range(first, last):
                far_move(i, up_sem, above).wait_recv()
                forward(i)

    relay(0, far)

    def from_z(d, carry):
        z = (ka + size_ka - d) % size_ka
        z_move(z, above).wait_recv()
        spread(z)
        return carry

    def from_plane(d, carry):
        z = (ka + size_ka - d) % size_ka

        def one(e, inner):
            c = (chip + chips - e) % chips
            plane_move(z, c, (chip + e) % chips).wait_recv()
            core_move(z, c, core).start()
            return inner

        return lax.fori_loop(1, chips, one, carry)

    for f in range(far):
        wide = far_form[f].astype(F32)
        source[f] = jnp.concatenate(
            [wide[:, h * LANES : (h + 1) * LANES] for h in range(pieces)], axis=0
        ).astype(BF16)

    def transfer(k, f):
        near_cell = grid_order[ka * near + k]
        far_cell = grid_order[kp * far + f]
        step_x = (near_cell // GRID_Y - far_cell // GRID_Y + grid_x) % grid_x
        step_y = (near_cell % GRID_Y - far_cell % GRID_Y + GRID_Y) % GRID_Y
        return step_x * GRID_Y + step_y

    z_steps = -(-(size_ka - 1) // 2)
    plane_steps = -(-size_ka // 4)
    first_plane = pairs - 5
    square = NV * NV

    def one_pair(n, carry):
        k, f = n // far, n % far
        q = transfer(k, f)
        total = jnp.zeros((square, NC * NC), F32)
        for s in range(0, waves, CHUNK):
            index = shift_map[pl.ds(q, 1), s : s + CHUNK]
            low = index & (LANES - 1)
            high = index // LANES
            one_hot = jnp.where(
                lax.broadcasted_iota(jnp.int32, (LANES, CHUNK), 0) == low, 1.0, 0.0
            ).astype(BF16)
            columns = jnp.dot(source[f], one_hot, preferred_element_type=F32)
            mapped = columns[0:bands]
            for h in range(1, pieces):
                mapped = jnp.where(high == h, columns[h * bands : (h + 1) * bands], mapped)
            near_form = form[k, :, s : s + CHUNK].astype(F32)
            valence = jnp.concatenate(
                [near_form[v : v + 1] * mapped[0:NV] for v in range(NV)], axis=0
            ).astype(BF16)
            conduction = jnp.concatenate(
                [near_form[NV + c : NV + c + 1] * mapped[NV:] for c in range(NC)], axis=0
            ).astype(BF16)
            valences[n, :, s : s + CHUNK] = valence
            conductions[n, :, s : s + CHUNK] = conduction
            scaled = (coulomb[:, s : s + CHUNK] * valence.astype(F32)).astype(BF16)
            total += lax.dot_general(scaled, conduction, NT, preferred_element_type=F32)
        direct[pl.ds(pl.multiple_of(n * square, square), square), :] = total

        @pl.when(n == 0)
        def _():
            relay(far, far + 2)

        @pl.when(n < 2)
        def _():
            low_d = 1 + n * z_steps
            lax.fori_loop(low_d, jnp.minimum(low_d + z_steps, size_ka), from_z, 0)

        @pl.when((n >= first_plane) & (n < first_plane + 4))
        def _():
            low_d = (n - first_plane) * plane_steps
            lax.fori_loop(low_d, jnp.minimum(low_d + plane_steps, size_ka), from_plane, 0)

        return carry

    lax.fori_loop(0, pairs, one_pair, 0)

    def finish(n, carry):
        z, c = n // chips, n % chips
        core_move(z, c, 1 - core).wait_recv()
        core_move(z, c, core).wait_send()
        return carry

    lax.fori_loop(0, size_ka * chips, finish, 0)

    def screening(n, carry):
        q = transfer(n // far, n % far)
        columns = all_cols[q // per_owner]
        left = jnp.dot(conductions[n], columns, preferred_element_type=F32)
        right = jnp.dot(valences[n], columns, preferred_element_type=F32)
        lane = lax.broadcasted_iota(jnp.int32, right.shape, 1)
        right = jnp.where(lane // group == q % per_owner, right, 0.0)
        at = pl.ds(pl.multiple_of(n * square, square), square)
        direct[at, :] += lax.dot_general(
            right, left, NT, precision=lax.Precision.HIGHEST, preferred_element_type=F32
        )
        return carry

    lax.fori_loop(0, pairs, screening, 0)

    all_rows = pairs * square
    row = lax.broadcasted_iota(jnp.int32, (all_rows, LANES), 0)
    lane = lax.broadcasted_iota(jnp.int32, (all_rows, LANES), 1)
    keep = row % NV == lane // NC
    sum_row = lax.broadcasted_iota(jnp.int32, (pairs * NV, all_rows), 0)
    sum_col = lax.broadcasted_iota(jnp.int32, (pairs * NV, all_rows), 1)
    sums = jnp.where(sum_col // NV == sum_row, 1.0, 0.0).astype(BF16)
    pick_row = lax.broadcasted_iota(jnp.int32, (LANES, LANES), 0)
    pick_lane = lax.broadcasted_iota(jnp.int32, (LANES, LANES), 1)
    per_half = LANES // NC
    for c in range(NC):
        pick = jnp.where(
            (pick_row // NC == c % per_half) & (pick_row % NC == pick_lane % NC), 1.0, 0.0
        ).astype(BF16)
        half_at = c // per_half * LANES
        wide = jnp.dot(
            direct[:, half_at : half_at + LANES].astype(BF16), pick, preferred_element_type=F32
        )
        wide = jnp.where(keep, wide, 0.0).astype(BF16)
        packed[pl.ds(c, pairs * NV, stride=NC), :] = jnp.dot(
            sums, wide, preferred_element_type=F32
        )
    for k in range(near):
        for f in range(far):
            at = (k * far + f) * side
            block = packed[at : at + side, :].astype(BF16)
            half = jnp.dot(block, far_coef[f], preferred_element_type=F32).astype(BF16)
            kernel[k * side : (k + 1) * side, f * side : (f + 1) * side] = lax.dot_general(
                coef[k], half, TN, preferred_element_type=F32
            ).astype(BF16)

    start[...] = initial[...].T
    vectors, rows = start.shape
    row_groups = vectors // 8
    lane_groups = size_kp // row_groups
    width = rows // lane_groups
    total_rows = rows * size_ka

    def chunk(p):
        return (
            pl.ds(pl.multiple_of(p // lane_groups * 8, 8), 8),
            pl.ds(pl.multiple_of(p % lane_groups * width, width), width),
        )

    own_rows, own_lanes = chunk(kp)
    padding = jnp.zeros((vectors, rows), F32)

    for step in range(STEPS):
        def rs_move(source, target):
            return pltpu.make_async_remote_copy(
                src_ref=product.at[step].at[chunk(target)],
                dst_ref=received.at[step, source],
                send_sem=rs_send.at[step, target], recv_sem=rs_recv.at[step, source],
                device_id={"kp": target}, device_id_type=MESH,
            )

        def ag_move(source, target):
            ref = image.at[step].at[chunk(source)]
            return pltpu.make_async_remote_copy(
                src_ref=ref, dst_ref=ref,
                send_sem=ag_send.at[step, target], recv_sem=ag_recv.at[step, source],
                device_id={"kp": target}, device_id_type=MESH,
            )

        def c_move(source, target):
            ref = correlations.at[step, source]
            return pltpu.make_async_remote_copy(
                src_ref=ref, dst_ref=ref,
                send_sem=c_send.at[step, target], recv_sem=c_recv.at[step, source],
                device_id={"ka": target}, device_id_type=MESH,
            )

        def image_move(target):
            return pltpu.make_async_remote_copy(
                src_ref=far_image.at[step], dst_ref=far_image.at[step],
                send_sem=far_send.at[step, target], recv_sem=far_recv.at[step],
                device_id={"ka": target}, device_id_type=MESH,
            )

        def loop(first, count, body):
            def one(d, carry):
                body(d)
                return carry

            lax.fori_loop(first, count, one, 0)

        total = jnp.zeros((vectors, rows), F32)
        for f in range(far):
            far_vectors = far_start[f] if step == 0 else far_bf16[f]
            total += lax.dot_general(
                far_vectors, kernel[:, f * side : (f + 1) * side], NT, preferred_element_type=F32
            )
        product[step] = total
        loop(1, size_kp, lambda d: rs_move(kp, (kp + d) % size_kp).start())
        received[step, kp] = product[step, own_rows, own_lanes]
        loop(1, size_kp, lambda d: rs_move((kp + size_kp - d) % size_kp, kp).wait_recv())
        value = energies[:, own_lanes] * start[own_rows, own_lanes]
        image[step, own_rows, own_lanes] = value + jnp.sum(received[step], axis=0)
        loop(1, size_kp, lambda d: ag_move(kp, (kp + d) % size_kp).start())
        loop(1, size_kp, lambda d: ag_move((kp + size_kp - d) % size_kp, kp).wait_recv())
        whole = image[step]
        correlations[step, ka] = lax.dot_general(
            whole, jnp.concatenate([whole, padding], axis=0), NT,
            precision=lax.Precision.HIGHEST, preferred_element_type=F32,
        )
        loop(1, size_ka, lambda d: c_move(ka, (ka + d) % size_ka).start())
        if step + 1 < STEPS:
            @pl.when(ka == owner)
            def _():
                for f in range(far):
                    far_image[step, f] = image[
                        step, :, pl.ds(pl.multiple_of((offset + f) * side, side), side)
                    ].astype(BF16)
                loop(1, size_ka, lambda d: image_move((ka + d) % size_ka).start())
        loop(1, size_ka, lambda d: c_move((ka + size_ka - d) % size_ka, ka).wait_recv())
        correlation = correlations[step, 0]
        for z in range(1, size_ka):
            correlation = correlation + correlations[step, z]
        inverse = inverse_factor(correlation * (1.0 / total_rows))
        start[...] = jnp.dot(
            inverse, jnp.concatenate([padding, whole], axis=0),
            precision=lax.Precision.HIGHEST, preferred_element_type=F32,
        )
        if step + 1 < STEPS:
            @pl.when(ka != owner)
            def _():
                image_move(ka).wait_recv()

            for f in range(far):
                far_bf16[f] = jnp.dot(
                    inverse,
                    jnp.concatenate([padding[:, :side], far_image[step, f].astype(F32)], axis=0),
                    precision=lax.Precision.HIGHEST, preferred_element_type=F32,
                ).astype(BF16)

            @pl.when(ka == owner)
            def _():
                loop(1, size_ka, lambda d: image_move((ka + d) % size_ka).wait_send())
        loop(1, size_kp, lambda d: rs_move(kp, (kp + d) % size_kp).wait_send())
        loop(1, size_kp, lambda d: ag_move(kp, (kp + d) % size_kp).wait_send())
        loop(1, size_ka, lambda d: c_move(ka, (ka + d) % size_ka).wait_send())

    subspace[...] = start[...].T

    def finish_plane(n, carry):
        z, e = n // (chips - 1), n % (chips - 1) + 1
        plane_move(z, chip, (chip + e) % chips).wait_send()
        return carry

    lax.fori_loop(0, size_ka * (chips - 1), finish_plane, 0)

    def finish_z(d, carry):
        z_move(ka, (ka + d) % size_ka).wait_send()
        return carry

    lax.fori_loop(1, size_ka, finish_z, 0)
    for i in range(len(sent)):
        @pl.when(goes_up)
        def _():
            far_move(i, up_sem, above).wait_send()

        @pl.when(goes_down)
        def _():
            far_move(i, down_sem, below).wait_send()


def on_device(band_form, interp_coef, screen, coulomb, shift_map, grid_order, energies, initial):
    size_ka = lax.axis_size("ka")
    size_kp = lax.axis_size("kp")
    near, bands, waves = band_form.shape
    side = interp_coef.shape[1]
    rows, vectors = initial.shape
    per_owner, _, group = screen.shape
    far = near * size_ka // size_kp
    pairs = near * far
    chips = size_kp // 2
    width = rows // (size_kp // (vectors // 8))
    dma = pltpu.SemaphoreType.DMA
    return pl.pallas_call(
        functools.partial(whole_kernel, size_ka, size_kp),
        out_shape=(
            jax.ShapeDtypeStruct((rows, far * side), BF16),
            jax.ShapeDtypeStruct((rows, vectors), F32),
        ),
        in_specs=[SMEM] + [VMEM] * 7,
        out_specs=(VMEM, VMEM),
        scratch_shapes=[
            pltpu.VMEM((far, bands, waves), BF16),
            pltpu.VMEM((far, side, side), BF16),
            pltpu.VMEM((far, vectors, side), BF16),
            pltpu.VMEM((size_ka, waves, per_owner * group), BF16),
            pltpu.VMEM((far, waves // LANES * bands, LANES), BF16),
            pltpu.VMEM((pairs, NC * NC, waves), BF16),
            pltpu.VMEM((pairs, NV * NV, waves), BF16),
            pltpu.VMEM((pairs * NV * NV, NC * NC), F32),
            pltpu.VMEM((pairs * side, LANES), F32),
            pltpu.VMEM((vectors, rows), F32),
            pltpu.VMEM((STEPS, vectors, rows), F32),
            pltpu.VMEM((STEPS, vectors, rows), F32),
            pltpu.VMEM((STEPS, far, vectors, side), BF16),
            pltpu.VMEM((far, vectors, side), BF16),
            pltpu.VMEM((STEPS, size_kp, 8, width), F32),
            pltpu.VMEM((STEPS, size_ka, vectors, 2 * vectors), F32),
            dma((far + 2,)), dma((far + 2,)), dma((far + 2,)),
            dma((size_ka,)), dma((size_ka,)),
            dma((size_ka, chips)), dma((size_ka, chips)),
            dma((size_ka, chips)), dma((size_ka, chips)),
            dma((STEPS, size_kp)), dma((STEPS, size_kp)),
            dma((STEPS, size_kp)), dma((STEPS, size_kp)),
            dma((STEPS, size_ka)), dma((STEPS, size_ka)),
            dma((STEPS, size_ka)), dma((STEPS,)),
        ],
        compiler_params=pltpu.CompilerParams(
            collective_id=0, has_side_effects=True, vmem_limit_bytes=56 * 2**20
        ),
    )(
        grid_order, band_form, interp_coef, screen, coulomb[None, :], shift_map,
        energies[None, :], initial,
    )


def solution(mesh):
    return jax.shard_map(
        on_device,
        mesh=mesh,
        in_specs=(
            P("ka", None, None),
            P("ka", None, None),
            P("ka", "kp", None),
            P(),
            P(),
            P(),
            P("ka"),
            P("ka", None),
        ),
        out_specs=(P("ka", "kp"), P("ka", None)),
        check_vma=False,
    )
```

time: 518 us -> 91.5 us (0.18)
  waiting for transfers between devices: 233 us -> 0 us
  Pallas kernels: 0 us -> 85.6 us
  local copies, waits for them, and re-layouts: 79.7 us -> 5.01 us
  blocking collectives: 53.8 us -> 0 us
  loops' own time: 47.7 us -> 0 us
  matrix products: 46.2 us -> 0 us
  other arithmetic: 36.6 us -> 0 us
  between operations: 14.1 us -> 0.66 us
    psum x4 -> x0, waiting for transfers between devices: 233 us -> none  [the longest x2 126 us: broadcast(): return lax.psum(block, axis)]
    pallas_call x0 -> x1, Pallas kernels: none -> 85.6 us  [on_device(): pl.pallas_call(functools.partial(whole_kernel, size_ka, size_kp), out_sha...]
    gather x20 -> x0, local copies, waits for them, and re-layouts: 53 us -> none  [the longest x16 51 us: one_pair(): mapped = jnp.take(far_form[far_slot], mapping, axis=1)]
    another operation x1 -> x0, loops' own time: 47.7 us -> none  [on_device(): blocks = lax.map(one_pair, (near_slots, far_slots, transfers, pair_screen))]
    dot_general x45 -> x0, matrix products: 43.1 us -> none  [the longest x8 11.8 us: pair_block(): left = jnp.dot(conduction, screen_cols, preferred_element_type=jnp.float32)]
    psum x2 -> x0, blocking collectives: 38 us -> none  [on_device(): correlation = lax.psum(local_correlation, 'ka') / (total_points * pairs)]
    another operation x10 -> x0, other arithmetic: 24.2 us -> none  [the longest x6 13 us: on_device(): factor = jnp.linalg.cholesky(correlation)]
    dynamic_slice x26 -> x0, local copies, waits for them, and re-layouts: 16.3 us -> none  [the longest x24 14.1 us: on_device(): blocks = lax.map(one_pair, (near_slots, far_slots, transfers, pair_screen))]
  transfers between devices with their start and end apart: 5 -> 0, of which waited for: 4 -> 0; matrix products, arithmetic and copies ran while one was open for 1% -> 0% of each run, Pallas kernels for 0% -> 0%
where the time goes in v2:
time: 91.5 us; the launch traced here: 91.3 us
  Pallas kernels  85.6 us (94%)
  local copies, waits for them, and re-layouts  5.01 us (5%)
    pallas_call x1, Pallas kernels, on_device(): pl.pallas_call(functools.partial(whole_kernel, size_ka, size_kp), out_sha...  85.6 us
    unnamed x7, local copies, waits for them, and re-layouts  3.25 us

profile of v2, /device:TPU:0, one launch (start us, length us, event | category | flops | bytes accessed | tf_op | source)
XLA Modules:
  0.0 91.3 jit_solution(8842428680748821657)
XLA Ops:
  0.6 0.0 copy-start.1
  0.6 1.7 %copy.10.screen = bf16[4,256,32]{2,1,0:T(8,128)(2,1)} copy(bf16[4,256,32]{1,2,0:T(8,128)(2,1)} %param.10) | data formatting | bytes 131072 | tf_op args[2]
  2.4 0.0 copy-done.1
  2.4 0.8 copy.11.initial
  3.2 85.6 %shard_map.95 = (bf16[512,256]{1,0:T(8,128)(2,1)}, f32[512,64]{1,0:T(8,128)}) custom-call(s32[16]{0:T(128)} %grid_order.1, bf16[4,24,2048]{2,1,0:T(8,128)(2,1)} %form.1, bf16[4,128,128]{2,1,0:T(8,128)(2,1)} %coef.1, bf16[4,256,32]{2,1,0:T(8,128)(2,1)} %copy.10.screen, f32[1,2048]{1,0:T(1,128)} %bitcast.2, s32[16,2048]{1,0:T(8,128)} %shift_map.1, ...), custom_call_target="tpu_custom_call" | custom-call | tf_op jit(solution)/shard_map/pallas_call | solution.py:443
  88.8 0.0 copy-start
  88.8 1.8 %copy.12 = f32[512,64]{0,1:T(8,128)} copy(f32[512,64]{1,0:T(8,128)} %get-tuple-element.3) | data formatting | bytes 262144 | tf_op jit(solution)/shard_map/pallas_call | solution.py:443
  90.6 0.0 copy-done
  90.6 0.7 copy.14
Async XLA Ops:
  0.6 1.7 %copy-start.1 = (f32[512,64]{0,1:T(8,128)S(1)}, f32[512,64]{0,1:T(8,128)}, u32[]{:S(2)}) copy-start(f32[512,64]{0,1:T(8,128)} %param.15) | copy-start | bytes 393220
  88.8 1.8 %copy-start = (bf16[512,256]{1,0:T(8,128)(2,1)S(1)}, bf16[512,256]{1,0:T(8,128)(2,1)}, u32[]{:S(2)}) copy-start(bf16[512,256]{1,0:T(8,128)(2,1)} %get-tuple-element.6) | copy-start | bytes 786436

commit v3 on v2

--- a/solution.py
+++ b/solution.py
@@ -12,7 +12,9 @@
 STEPS = 2
 GRID_Y = 8
 LANES = 128
+DEPTH = 256
 CHUNK = 512
+SUB = 16
 MESH = pl.DeviceIdType.MESH
 VMEM = pl.BlockSpec(memory_space=pltpu.VMEM)
 SMEM = pl.BlockSpec(memory_space=pltpu.SMEM)
@@ -27,10 +29,15 @@
     row = lax.broadcasted_iota(jnp.int32, matrix.shape, 0)
     lane = lax.broadcasted_iota(jnp.int32, matrix.shape, 1)
     work = jnp.where(lane == row + size, 1.0, matrix)
-    for j in range(size - 1):
-        pivot_row = work[j : j + 1, :]
-        scaled_row = pivot_row / pivot_row[:, j : j + 1]
-        work = work - jnp.where(row > j, work[:, j : j + 1], 0.0) * scaled_row
+    for j in range(0, size, 2):
+        first, second = work[j : j + 1, :], work[j + 1 : j + 2, :]
+        first_inverse = 1.0 / first[:, j : j + 1]
+        ratio = second[:, j : j + 1] * first_inverse
+        second = second - ratio * first
+        second_scaled = second * (1.0 / second[:, j + 1 : j + 2])
+        first_scaled = first * first_inverse - ratio * second_scaled
+        update = work[:, j : j + 1] * first_scaled + work[:, j + 1 : j + 2] * second_scaled
+        work = jnp.where(row > j + 1, work - update, jnp.where(row == j + 1, second, work))
     diagonal = jnp.sum(jnp.where(lane == row, work, 0.0), axis=1, keepdims=True)
     return jnp.where(lane >= size, work * lax.rsqrt(diagonal), 0.0)
 
@@ -39,7 +46,7 @@
     size_ka, size_kp,
     grid_order, form, coef, screen, coulomb, shift_map, energies, initial,
     kernel, subspace,
-    far_form, far_coef, far_start, all_cols, source, conductions, valences, direct, packed, start,
+    far_form, far_coef, far_start, all_cols, source, near_rows, conductions, valences, direct, packed, start,
     product, image, far_image, far_bf16, received, correlations,
     up_sem, down_sem, far_sem, z_send, z_recv, plane_send, plane_recv, core_send, core_recv,
     rs_send, rs_recv, ag_send, ag_recv, c_send, c_recv, far_send, far_recv,
@@ -50,9 +57,9 @@
     near, far = form.shape[0], far_form.shape[0]
     owner = kp * far // near
     offset = kp * far % near
-    per_owner, cut, group = screen.shape
+    per_owner, group, cut = screen.shape
     waves = form.shape[2]
-    pieces = waves // LANES
+    pieces = waves // DEPTH
     bands = NV + NC
     side = NV * NC
     pairs = near * far
@@ -76,18 +83,25 @@
         far_form[...] = form[pl.ds(offset, far)]
         far_coef[...] = coef[pl.ds(offset, far)]
         for f in range(far):
-            rows = pl.ds(pl.multiple_of((offset + f) * side, side), side)
-            far_start[f] = initial[rows, :].T.astype(BF16)
+            far_start[f] = initial[
+                :, pl.ds(pl.multiple_of((offset + f) * side, side), side)
+            ].astype(BF16)
 
     def part(z, p):
         return all_cols.at[z, pl.ds(pl.multiple_of(p * cut, cut), cut), :]
 
-    all_cols[ka, pl.ds(pl.multiple_of(kp * cut, cut), cut), :] = jnp.concatenate(
-        [screen[n] for n in range(per_owner)], axis=1
+    all_cols[ka, pl.ds(pl.multiple_of(kp * cut, cut), cut), :] = (
+        screen[...].reshape(per_owner * group, cut).astype(F32).T.astype(BF16)
     )
     pl.semaphore_wait(barrier, size_ka - 1 + size_kp - 1)
 
-    sent = [far_form.at[i] for i in range(far)] + [far_coef, far_start]
+    half_waves = waves // 2
+    sent = [
+        far_form.at[f, :, h * half_waves : (h + 1) * half_waves]
+        for f in range(far)
+        for h in range(2)
+    ] + [far_coef, far_start]
+    forms = 2 * far
 
     def far_move(i, sem, target):
         return pltpu.make_async_remote_copy(
@@ -142,12 +156,21 @@
         for i in range(len(sent)):
             forward(i)
 
-    def to_z(d, carry):
-        z_move(ka, (ka + d) % size_ka).start()
-        return carry
-
-    lax.fori_loop(1, size_ka, to_z, 0)
     spread(ka)
+
+    def spread_near(k, carry):
+        wide = form[k].astype(F32)
+        for v in range(0, NV, 2):
+            near_rows[k, v // 2] = jnp.concatenate(
+                [jnp.broadcast_to(wide[v + i : v + i + 1], (NV, waves)) for i in range(2)], axis=0
+            ).astype(BF16)
+        for c in range(NC):
+            near_rows[k, NV // 2 + c] = jnp.broadcast_to(
+                wide[NV + c : NV + c + 1], (NC, waves)
+            ).astype(BF16)
+        return carry
+
+    lax.fori_loop(0, near, spread_near, 0)
 
     def relay(first, last):
         @pl.when(ka != owner)
@@ -156,7 +179,13 @@
                 far_move(i, up_sem, above).wait_recv()
                 forward(i)
 
-    relay(0, far)
+    relay(0, forms)
+
+    def to_z(d, carry):
+        z_move(ka, (ka + d) % size_ka).start()
+        return carry
+
+    lax.fori_loop(1, size_ka, to_z, 0)
 
     def from_z(d, carry):
         z = (ka + size_ka - d) % size_ka
@@ -178,7 +207,7 @@
     for f in range(far):
         wide = far_form[f].astype(F32)
         source[f] = jnp.concatenate(
-            [wide[:, h * LANES : (h + 1) * LANES] for h in range(pieces)], axis=0
+            [wide[:, h * DEPTH : (h + 1) * DEPTH] for h in range(pieces)], axis=0
         ).astype(BF16)
 
     def transfer(k, f):
@@ -193,28 +222,37 @@
     first_plane = pairs - 5
     square = NV * NV
 
+    steps = lax.broadcasted_iota(jnp.int32, (SUB, CHUNK), 0)
+    one, zero = jnp.ones((SUB, CHUNK), BF16), jnp.zeros((SUB, CHUNK), BF16)
+
     def one_pair(n, carry):
         k, f = n // far, n % far
         q = transfer(k, f)
         total = jnp.zeros((square, NC * NC), F32)
         for s in range(0, waves, CHUNK):
             index = shift_map[pl.ds(q, 1), s : s + CHUNK]
-            low = index & (LANES - 1)
-            high = index // LANES
-            one_hot = jnp.where(
-                lax.broadcasted_iota(jnp.int32, (LANES, CHUNK), 0) == low, 1.0, 0.0
-            ).astype(BF16)
+            low = jnp.broadcast_to(index % DEPTH, (SUB, CHUNK)).astype(F32).astype(BF16)
+            high = index // DEPTH
+            one_hot = jnp.concatenate(
+                [
+                    jnp.where((steps + r).astype(F32).astype(BF16) == low, one, zero)
+                    for r in range(0, DEPTH, SUB)
+                ],
+                axis=0,
+            )
             columns = jnp.dot(source[f], one_hot, preferred_element_type=F32)
             mapped = columns[0:bands]
             for h in range(1, pieces):
                 mapped = jnp.where(high == h, columns[h * bands : (h + 1) * bands], mapped)
-            near_form = form[k, :, s : s + CHUNK].astype(F32)
+            top = mapped[0:NV]
+            top = jnp.concatenate([top, top], axis=0).astype(BF16)
+            rest = mapped[NV:].astype(BF16)
             valence = jnp.concatenate(
-                [near_form[v : v + 1] * mapped[0:NV] for v in range(NV)], axis=0
-            ).astype(BF16)
+                [near_rows[k, i, :, s : s + CHUNK] * top for i in range(NV // 2)], axis=0
+            )
             conduction = jnp.concatenate(
-                [near_form[NV + c : NV + c + 1] * mapped[NV:] for c in range(NC)], axis=0
-            ).astype(BF16)
+                [near_rows[k, NV // 2 + c, :, s : s + CHUNK] * rest for c in range(NC)], axis=0
+            )
             valences[n, :, s : s + CHUNK] = valence
             conductions[n, :, s : s + CHUNK] = conduction
             scaled = (coulomb[:, s : s + CHUNK] * valence.astype(F32)).astype(BF16)
@@ -223,7 +261,7 @@
 
         @pl.when(n == 0)
         def _():
-            relay(far, far + 2)
+            relay(forms, forms + 2)
 
         @pl.when(n < 2)
         def _():
@@ -247,20 +285,22 @@
 
     lax.fori_loop(0, size_ka * chips, finish, 0)
 
-    def screening(n, carry):
-        q = transfer(n // far, n % far)
-        columns = all_cols[q // per_owner]
-        left = jnp.dot(conductions[n], columns, preferred_element_type=F32)
-        right = jnp.dot(valences[n], columns, preferred_element_type=F32)
-        lane = lax.broadcasted_iota(jnp.int32, right.shape, 1)
-        right = jnp.where(lane // group == q % per_owner, right, 0.0)
-        at = pl.ds(pl.multiple_of(n * square, square), square)
-        direct[at, :] += lax.dot_general(
-            right, left, NT, precision=lax.Precision.HIGHEST, preferred_element_type=F32
-        )
-        return carry
-
-    lax.fori_loop(0, pairs, screening, 0)
+    def screening(k, carry):
+        for f in range(far):
+            n = k * far + f
+            q = transfer(k, f)
+            columns = all_cols[q // per_owner]
+            left = jnp.dot(conductions[n], columns, preferred_element_type=F32)
+            right = jnp.dot(valences[n], columns, preferred_element_type=F32)
+            lane = lax.broadcasted_iota(jnp.int32, right.shape, 1)
+            right = jnp.where(lane // group == q % per_owner, right, 0.0)
+            at = pl.ds(pl.multiple_of(n * square, square), square)
+            direct[at, :] += lax.dot_general(
+                right.astype(BF16), left.astype(BF16), NT, preferred_element_type=F32
+            )
+        return carry
+
+    lax.fori_loop(0, near, screening, 0)
 
     all_rows = pairs * square
     row = lax.broadcasted_iota(jnp.int32, (all_rows, LANES), 0)
@@ -293,7 +333,7 @@
                 coef[k], half, TN, preferred_element_type=F32
             ).astype(BF16)
 
-    start[...] = initial[...].T
+    start[...] = initial[...]
     vectors, rows = start.shape
     row_groups = vectors // 8
     lane_groups = size_kp // row_groups
@@ -404,7 +444,7 @@
         loop(1, size_kp, lambda d: ag_move(kp, (kp + d) % size_kp).wait_send())
         loop(1, size_ka, lambda d: c_move(ka, (ka + d) % size_ka).wait_send())
 
-    subspace[...] = start[...].T
+    subspace[...] = start[...]
 
     def finish_plane(n, carry):
         z, e = n // (chips - 1), n % (chips - 1) + 1
@@ -440,11 +480,11 @@
     chips = size_kp // 2
     width = rows // (size_kp // (vectors // 8))
     dma = pltpu.SemaphoreType.DMA
-    return pl.pallas_call(
+    kernel, subspace = pl.pallas_call(
         functools.partial(whole_kernel, size_ka, size_kp),
         out_shape=(
             jax.ShapeDtypeStruct((rows, far * side), BF16),
-            jax.ShapeDtypeStruct((rows, vectors), F32),
+            jax.ShapeDtypeStruct((vectors, rows), F32),
         ),
         in_specs=[SMEM] + [VMEM] * 7,
         out_specs=(VMEM, VMEM),
@@ -453,7 +493,8 @@
             pltpu.VMEM((far, side, side), BF16),
             pltpu.VMEM((far, vectors, side), BF16),
             pltpu.VMEM((size_ka, waves, per_owner * group), BF16),
-            pltpu.VMEM((far, waves // LANES * bands, LANES), BF16),
+            pltpu.VMEM((far, waves // DEPTH * bands, DEPTH), BF16),
+            pltpu.VMEM((near, NV // 2 + NC, SUB, waves), BF16),
             pltpu.VMEM((pairs, NC * NC, waves), BF16),
             pltpu.VMEM((pairs, NV * NV, waves), BF16),
             pltpu.VMEM((pairs * NV * NV, NC * NC), F32),
@@ -465,7 +506,7 @@
             pltpu.VMEM((far, vectors, side), BF16),
             pltpu.VMEM((STEPS, size_kp, 8, width), F32),
             pltpu.VMEM((STEPS, size_ka, vectors, 2 * vectors), F32),
-            dma((far + 2,)), dma((far + 2,)), dma((far + 2,)),
+            dma((2 * far + 2,)), dma((2 * far + 2,)), dma((2 * far + 2,)),
             dma((size_ka,)), dma((size_ka,)),
             dma((size_ka, chips)), dma((size_ka, chips)),
             dma((size_ka, chips)), dma((size_ka, chips)),
@@ -478,9 +519,10 @@
             collective_id=0, has_side_effects=True, vmem_limit_bytes=56 * 2**20
         ),
     )(
-        grid_order, band_form, interp_coef, screen, coulomb[None, :], shift_map,
-        energies[None, :], initial,
+        grid_order, band_form, interp_coef, screen.transpose(0, 2, 1), coulomb[None, :], shift_map,
+        energies[None, :], initial.T,
     )
+    return kernel, subspace.T
 
 
 def solution(mesh):

time: 91.5 us -> 86.9 us (0.950)
  local copies, waits for them, and re-layouts: 5.01 us -> 2.36 us
  Pallas kernels: 85.6 us -> 83.7 us
    pallas_call x1, Pallas kernels: 85.6 us -> 83.7 us  [on_device(): pl.pallas_call(functools.partial(whole_kernel, size_ka, size_kp), out_sha...]
    pallas_call x1 -> x0, local copies, waits for them, and re-layouts: 1.76 us -> none  [on_device(): pl.pallas_call(functools.partial(whole_kernel, size_ka, size_kp), out_sha...]
    unnamed x7 -> x4, local copies, waits for them, and re-layouts: 3.25 us -> 2.36 us
where the time goes in v3:
time: 86.9 us; the launch traced here: 86.7 us
  Pallas kernels  83.7 us (96%)
  local copies, waits for them, and re-layouts  2.36 us (3%)
    pallas_call x1, Pallas kernels, on_device(): pl.pallas_call(functools.partial(whole_kernel, size_ka, size_kp), out_sha...  83.7 us
    unnamed x4, local copies, waits for them, and re-layouts  2.36 us

profile of v3, /device:TPU:0, one launch (start us, length us, event | category | flops | bytes accessed | tf_op | source)
XLA Modules:
  0.0 86.7 jit_solution(6713425498505899896)
XLA Ops:
  0.6 83.7 %shard_map.95 = (bf16[512,256]{1,0:T(8,128)(2,1)}, f32[64,512]{1,0:T(8,128)}) custom-call(s32[16]{0:T(128)} %grid_order.1, bf16[4,24,2048]{2,1,0:T(8,128)(2,1)} %form.1, bf16[4,128,128]{2,1,0:T(8,128)(2,1)} %coef.1, bf16[4,32,256]{2,1,0:T(8,128)(2,1)} %bitcast.7, f32[1,2048]{1,0:T(1,128)} %bitcast.8, s32[16,2048]{1,0:T(8,128)} %shift_map.1, ...), custom_call_target="tpu_custom_call" | custom-call | tf_op jit(solution)/shard_map/pallas_call | solution.py:483
  84.3 0.0 copy-start
  84.4 1.7 %copy.12 = bf16[512,256]{1,0:T(8,128)(2,1)} copy(bf16[512,256]{1,0:T(8,128)(2,1)} %get-tuple-element.8) | data formatting | bytes 524288
  86.1 0.0 copy-done
  86.1 0.7 copy.13
Async XLA Ops:
  84.3 1.7 %copy-start = (f32[64,512]{1,0:T(8,128)S(1)}, f32[64,512]{1,0:T(8,128)}, u32[]{:S(2)}) copy-start(f32[64,512]{1,0:T(8,128)} %get-tuple-element.5) | copy-start | bytes 393220

commit v4 on v3

--- a/solution.py
+++ b/solution.py
@@ -15,6 +15,7 @@
 DEPTH = 256
 CHUNK = 512
 SUB = 16
+COPIES = 4
 MESH = pl.DeviceIdType.MESH
 VMEM = pl.BlockSpec(memory_space=pltpu.VMEM)
 SMEM = pl.BlockSpec(memory_space=pltpu.SMEM)
@@ -24,11 +25,16 @@
 BF16 = jnp.bfloat16
 
 
+def log2(size):
+    return size.bit_length() - 1
+
+
 def inverse_factor(matrix):
     size = matrix.shape[0]
-    row = lax.broadcasted_iota(jnp.int32, matrix.shape, 0)
-    lane = lax.broadcasted_iota(jnp.int32, matrix.shape, 1)
-    work = jnp.where(lane == row + size, 1.0, matrix)
+    work = jnp.concatenate([matrix, jnp.zeros_like(matrix)], axis=1)
+    row = lax.broadcasted_iota(jnp.int32, work.shape, 0)
+    lane = lax.broadcasted_iota(jnp.int32, work.shape, 1)
+    work = jnp.where(lane == row + size, 1.0, work)
     for j in range(0, size, 2):
         first, second = work[j : j + 1, :], work[j + 1 : j + 2, :]
         first_inverse = 1.0 / first[:, j : j + 1]
@@ -46,7 +52,7 @@
     size_ka, size_kp,
     grid_order, form, coef, screen, coulomb, shift_map, energies, initial,
     kernel, subspace,
-    far_form, far_coef, far_start, all_cols, source, near_rows, conductions, valences, direct, packed, start,
+    far_form, far_coef, far_start, all_cols, source, near_rows, conductions, valences, direct, packed, inverse_rows,
     product, image, far_image, far_bf16, received, correlations,
     up_sem, down_sem, far_sem, z_send, z_recv, plane_send, plane_recv, core_send, core_recv,
     rs_send, rs_recv, ag_send, ag_recv, c_send, c_recv, far_send, far_recv,
@@ -179,7 +185,7 @@
                 far_move(i, up_sem, above).wait_recv()
                 forward(i)
 
-    relay(0, forms)
+    relay(0, 2)
 
     def to_z(d, carry):
         z_move(ka, (ka + d) % size_ka).start()
@@ -204,11 +210,13 @@
 
         return lax.fori_loop(1, chips, one, carry)
 
-    for f in range(far):
+    def stack(f):
         wide = far_form[f].astype(F32)
         source[f] = jnp.concatenate(
             [wide[:, h * DEPTH : (h + 1) * DEPTH] for h in range(pieces)], axis=0
         ).astype(BF16)
+
+    stack(0)
 
     def transfer(k, f):
         near_cell = grid_order[ka * near + k]
@@ -226,13 +234,14 @@
     one, zero = jnp.ones((SUB, CHUNK), BF16), jnp.zeros((SUB, CHUNK), BF16)
 
     def one_pair(n, carry):
-        k, f = n // far, n % far
+        f, k = n // near, n % near
+        slot = k * far + f
         q = transfer(k, f)
         total = jnp.zeros((square, NC * NC), F32)
         for s in range(0, waves, CHUNK):
             index = shift_map[pl.ds(q, 1), s : s + CHUNK]
-            low = jnp.broadcast_to(index % DEPTH, (SUB, CHUNK)).astype(F32).astype(BF16)
-            high = index // DEPTH
+            low = jnp.broadcast_to(index & (DEPTH - 1), (SUB, CHUNK)).astype(F32).astype(BF16)
+            high = index >> log2(DEPTH)
             one_hot = jnp.concatenate(
                 [
                     jnp.where((steps + r).astype(F32).astype(BF16) == low, one, zero)
@@ -253,19 +262,25 @@
             conduction = jnp.concatenate(
                 [near_rows[k, NV // 2 + c, :, s : s + CHUNK] * rest for c in range(NC)], axis=0
             )
-            valences[n, :, s : s + CHUNK] = valence
-            conductions[n, :, s : s + CHUNK] = conduction
+            valences[slot, :, s : s + CHUNK] = valence
+            conductions[slot, :, s : s + CHUNK] = conduction
             scaled = (coulomb[:, s : s + CHUNK] * valence.astype(F32)).astype(BF16)
             total += lax.dot_general(scaled, conduction, NT, preferred_element_type=F32)
-        direct[pl.ds(pl.multiple_of(n * square, square), square), :] = total
-
-        @pl.when(n == 0)
+        direct[pl.ds(pl.multiple_of(slot * square, square), square), :] = total
+
+        for after in range(1, far):
+            @pl.when(n == after - 1)
+            def _():
+                relay(2 * after, 2 * after + 2)
+                stack(after)
+
+        @pl.when(n == far - 1)
         def _():
             relay(forms, forms + 2)
 
-        @pl.when(n < 2)
-        def _():
-            low_d = 1 + n * z_steps
+        @pl.when((n >= 1) & (n < 3))
+        def _():
+            low_d = 1 + (n - 1) * z_steps
             lax.fori_loop(low_d, jnp.minimum(low_d + z_steps, size_ka), from_z, 0)
 
         @pl.when((n >= first_plane) & (n < first_plane + 4))
@@ -293,7 +308,7 @@
             left = jnp.dot(conductions[n], columns, preferred_element_type=F32)
             right = jnp.dot(valences[n], columns, preferred_element_type=F32)
             lane = lax.broadcasted_iota(jnp.int32, right.shape, 1)
-            right = jnp.where(lane // group == q % per_owner, right, 0.0)
+            right = jnp.where((lane >> log2(group)) == q % per_owner, right, 0.0)
             at = pl.ds(pl.multiple_of(n * square, square), square)
             direct[at, :] += lax.dot_general(
                 right.astype(BF16), left.astype(BF16), NT, preferred_element_type=F32
@@ -305,16 +320,17 @@
     all_rows = pairs * square
     row = lax.broadcasted_iota(jnp.int32, (all_rows, LANES), 0)
     lane = lax.broadcasted_iota(jnp.int32, (all_rows, LANES), 1)
-    keep = row % NV == lane // NC
+    keep = (row & (NV - 1)) == (lane >> log2(NC))
     sum_row = lax.broadcasted_iota(jnp.int32, (pairs * NV, all_rows), 0)
     sum_col = lax.broadcasted_iota(jnp.int32, (pairs * NV, all_rows), 1)
-    sums = jnp.where(sum_col // NV == sum_row, 1.0, 0.0).astype(BF16)
+    sums = jnp.where((sum_col >> log2(NV)) == sum_row, 1.0, 0.0).astype(BF16)
     pick_row = lax.broadcasted_iota(jnp.int32, (LANES, LANES), 0)
     pick_lane = lax.broadcasted_iota(jnp.int32, (LANES, LANES), 1)
     per_half = LANES // NC
+    same = (pick_row & (NC - 1)) == (pick_lane & (NC - 1))
     for c in range(NC):
         pick = jnp.where(
-            (pick_row // NC == c % per_half) & (pick_row % NC == pick_lane % NC), 1.0, 0.0
+            ((pick_row >> log2(NC)) == c % per_half) & same, 1.0, 0.0
         ).astype(BF16)
         half_at = c // per_half * LANES
         wide = jnp.dot(
@@ -333,8 +349,8 @@
                 coef[k], half, TN, preferred_element_type=F32
             ).astype(BF16)
 
-    start[...] = initial[...]
-    vectors, rows = start.shape
+    vectors, rows = initial.shape
+    half = vectors // 2
     row_groups = vectors // 8
     lane_groups = size_kp // row_groups
     width = rows // lane_groups
@@ -397,16 +413,26 @@
         product[step] = total
         loop(1, size_kp, lambda d: rs_move(kp, (kp + d) % size_kp).start())
         received[step, kp] = product[step, own_rows, own_lanes]
+        if step == 0:
+            current = initial[own_rows, own_lanes]
+        else:
+            current = jnp.dot(
+                inverse_rows[own_rows, :],
+                jnp.concatenate(
+                    [padding[:, :width], image[step - 1, :, own_lanes]], axis=0
+                ),
+                precision=lax.Precision.HIGHEST, preferred_element_type=F32,
+            )
         loop(1, size_kp, lambda d: rs_move((kp + size_kp - d) % size_kp, kp).wait_recv())
-        value = energies[:, own_lanes] * start[own_rows, own_lanes]
+        value = energies[:, own_lanes] * current
         image[step, own_rows, own_lanes] = value + jnp.sum(received[step], axis=0)
         loop(1, size_kp, lambda d: ag_move(kp, (kp + d) % size_kp).start())
         loop(1, size_kp, lambda d: ag_move((kp + size_kp - d) % size_kp, kp).wait_recv())
         whole = image[step]
-        correlations[step, ka] = lax.dot_general(
-            whole, jnp.concatenate([whole, padding], axis=0), NT,
-            precision=lax.Precision.HIGHEST, preferred_element_type=F32,
-        )
+        local = lax.dot_general(
+            whole, whole, NT, precision=lax.Precision.HIGHEST, preferred_element_type=F32
+        )
+        correlations[step, ka] = jnp.concatenate([local[:half], local[half:]], axis=1)
         loop(1, size_ka, lambda d: c_move(ka, (ka + d) % size_ka).start())
         if step + 1 < STEPS:
             @pl.when(ka == owner)
@@ -414,17 +440,21 @@
                 for f in range(far):
                     far_image[step, f] = image[
                         step, :, pl.ds(pl.multiple_of((offset + f) * side, side), side)
-                    ].astype(BF16)
+                    ]
                 loop(1, size_ka, lambda d: image_move((ka + d) % size_ka).start())
         loop(1, size_ka, lambda d: c_move((ka + size_ka - d) % size_ka, ka).wait_recv())
         correlation = correlations[step, 0]
         for z in range(1, size_ka):
             correlation = correlation + correlations[step, z]
+        correlation = jnp.concatenate([correlation[:, :vectors], correlation[:, vectors:]], axis=0)
         inverse = inverse_factor(correlation * (1.0 / total_rows))
-        start[...] = jnp.dot(
-            inverse, jnp.concatenate([padding, whole], axis=0),
-            precision=lax.Precision.HIGHEST, preferred_element_type=F32,
-        )
+        if step + 1 < STEPS:
+            inverse_rows[...] = inverse
+        else:
+            subspace[...] = jnp.dot(
+                inverse, jnp.concatenate([padding, whole], axis=0),
+                precision=lax.Precision.HIGHEST, preferred_element_type=F32,
+            )
         if step + 1 < STEPS:
             @pl.when(ka != owner)
             def _():
@@ -433,7 +463,7 @@
             for f in range(far):
                 far_bf16[f] = jnp.dot(
                     inverse,
-                    jnp.concatenate([padding[:, :side], far_image[step, f].astype(F32)], axis=0),
+                    jnp.concatenate([padding[:, :side], far_image[step, f]], axis=0),
                     precision=lax.Precision.HIGHEST, preferred_element_type=F32,
                 ).astype(BF16)
 
@@ -444,8 +474,6 @@
         loop(1, size_kp, lambda d: ag_move(kp, (kp + d) % size_kp).wait_send())
         loop(1, size_ka, lambda d: c_move(ka, (ka + d) % size_ka).wait_send())
 
-    subspace[...] = start[...]
-
     def finish_plane(n, carry):
         z, e = n // (chips - 1), n % (chips - 1) + 1
         plane_move(z, chip, (chip + e) % chips).wait_send()
@@ -466,6 +494,31 @@
         @pl.when(goes_down)
         def _():
             far_move(i, down_sem, below).wait_send()
+
+
+def hand_over_kernel(kernel, subspace, kernel_out, subspace_out, sems):
+    rows = kernel.shape[0] // COPIES
+    moves = [
+        pltpu.make_async_copy(
+            kernel.at[pl.ds(i * rows, rows)], kernel_out.at[pl.ds(i * rows, rows)], sems.at[i]
+        )
+        for i in range(COPIES)
+    ] + [pltpu.make_async_copy(subspace, subspace_out, sems.at[COPIES])]
+    for move in moves:
+        move.start()
+    for move in moves:
+        move.wait()
+
+
+def hand_over(kernel, subspace):
+    anywhere = pl.BlockSpec(memory_space=pl.ANY)
+    return pl.pallas_call(
+        hand_over_kernel,
+        out_shape=tuple(jax.ShapeDtypeStruct(x.shape, x.dtype) for x in (kernel, subspace)),
+        in_specs=[anywhere, anywhere],
+        out_specs=(anywhere, anywhere),
+        scratch_shapes=[pltpu.SemaphoreType.DMA((COPIES + 1,))],
+    )(kernel, subspace)
 
 
 def on_device(band_form, interp_coef, screen, coulomb, shift_map, grid_order, energies, initial):
@@ -499,13 +552,13 @@
             pltpu.VMEM((pairs, NV * NV, waves), BF16),
             pltpu.VMEM((pairs * NV * NV, NC * NC), F32),
             pltpu.VMEM((pairs * side, LANES), F32),
-            pltpu.VMEM((vectors, rows), F32),
+            pltpu.VMEM((vectors, 2 * vectors), F32),
             pltpu.VMEM((STEPS, vectors, rows), F32),
             pltpu.VMEM((STEPS, vectors, rows), F32),
-            pltpu.VMEM((STEPS, far, vectors, side), BF16),
+            pltpu.VMEM((STEPS, far, vectors, side), F32),
             pltpu.VMEM((far, vectors, side), BF16),
             pltpu.VMEM((STEPS, size_kp, 8, width), F32),
-            pltpu.VMEM((STEPS, size_ka, vectors, 2 * vectors), F32),
+            pltpu.VMEM((STEPS, size_ka, vectors // 2, 2 * vectors), F32),
             dma((2 * far + 2,)), dma((2 * far + 2,)), dma((2 * far + 2,)),
             dma((size_ka,)), dma((size_ka,)),
             dma((size_ka, chips)), dma((size_ka, chips)),
@@ -522,6 +575,7 @@
         grid_order, band_form, interp_coef, screen.transpose(0, 2, 1), coulomb[None, :], shift_map,
         energies[None, :], initial.T,
     )
+    kernel, subspace = hand_over(kernel, subspace)
     return kernel, subspace.T
 
 

time: 86.9 us -> 96.6 us (1.11)
  Pallas kernels: 83.7 us -> 95.8 us
  local copies, waits for them, and re-layouts: 2.36 us -> 0 us
    pallas_call x0 -> x1, Pallas kernels: none -> 13.1 us  [hand_over(): pl.pallas_call(hand_over_kernel, out_shape=tuple((jax.ShapeDtypeStruct(x....]
    unnamed x4 -> x0, local copies, waits for them, and re-layouts: 2.36 us -> none
    pallas_call x1, Pallas kernels: 83.7 us -> 82.7 us  [on_device(): pl.pallas_call(functools.partial(whole_kernel, size_ka, size_kp), out_sha...]
where the time goes in v4:
time: 96.6 us; the launch traced here: 96.4 us
  Pallas kernels  95.8 us (99%)
    pallas_call x1, Pallas kernels, on_device(): pl.pallas_call(functools.partial(whole_kernel, size_ka, size_kp), out_sha...  82.7 us
    pallas_call x1, Pallas kernels, hand_over(): pl.pallas_call(hand_over_kernel, out_shape=tuple((jax.ShapeDtypeStruct(x....  13.1 us

profile of v4, /device:TPU:0, one launch (start us, length us, event | category | flops | bytes accessed | tf_op | source)
XLA Modules:
  0.0 96.4 jit_solution(6245674264270897494)
XLA Ops:
  0.6 82.7 %shard_map.95 = (bf16[512,256]{1,0:T(8,128)(2,1)}, f32[64,512]{1,0:T(8,128)}) custom-call(s32[16]{0:T(128)} %grid_order.1, bf16[4,24,2048]{2,1,0:T(8,128)(2,1)} %form.1, bf16[4,128,128]{2,1,0:T(8,128)(2,1)} %coef.1, bf16[4,32,256]{2,1,0:T(8,128)(2,1)} %bitcast.6, f32[1,2048]{1,0:T(1,128)} %bitcast.7, s32[16,2048]{1,0:T(8,128)} %shift_map.1, ...), custom_call_target="tpu_custom_call" | custom-call | tf_op jit(solution)/shard_map/pallas_call | solution.py:536
  83.3 13.1 %shard_map.96 = (bf16[512,256]{1,0:T(8,128)(2,1)}, f32[64,512]{1,0:T(8,128)}) custom-call(bf16[512,256]{1,0:T(8,128)(2,1)} %get-tuple-element.6.kernel, f32[64,512]{1,0:T(8,128)} %get-tuple-element.7.subspace), custom_call_target="tpu_custom_call" | custom-call | tf_op jit(solution)/shard_map/pallas_call | solution.py:515

commit v5 on v4

--- a/solution.py
+++ b/solution.py
@@ -15,7 +15,6 @@
 DEPTH = 256
 CHUNK = 512
 SUB = 16
-COPIES = 4
 MESH = pl.DeviceIdType.MESH
 VMEM = pl.BlockSpec(memory_space=pltpu.VMEM)
 SMEM = pl.BlockSpec(memory_space=pltpu.SMEM)
@@ -159,8 +158,14 @@
 
     @pl.when(ka == owner)
     def _():
-        for i in range(len(sent)):
+        for i in range(forms):
             forward(i)
+
+    def to_z(d, carry):
+        z_move(ka, (ka + d) % size_ka).start()
+        return carry
+
+    lax.fori_loop(1, size_ka, to_z, 0)
 
     spread(ka)
 
@@ -187,12 +192,6 @@
 
     relay(0, 2)
 
-    def to_z(d, carry):
-        z_move(ka, (ka + d) % size_ka).start()
-        return carry
-
-    lax.fori_loop(1, size_ka, to_z, 0)
-
     def from_z(d, carry):
         z = (ka + size_ka - d) % size_ka
         z_move(z, above).wait_recv()
@@ -217,6 +216,7 @@
         ).astype(BF16)
 
     stack(0)
+    lax.fori_loop(1, size_ka, from_z, 0)
 
     def transfer(k, f):
         near_cell = grid_order[ka * near + k]
@@ -225,9 +225,8 @@
         step_y = (near_cell % GRID_Y - far_cell % GRID_Y + GRID_Y) % GRID_Y
         return step_x * GRID_Y + step_y
 
-    z_steps = -(-(size_ka - 1) // 2)
     plane_steps = -(-size_ka // 4)
-    first_plane = pairs - 5
+    first_plane = pairs - 6
     square = NV * NV
 
     steps = lax.broadcasted_iota(jnp.int32, (SUB, CHUNK), 0)
@@ -276,12 +275,12 @@
 
         @pl.when(n == far - 1)
         def _():
+            @pl.when(ka == owner)
+            def _():
+                for i in range(forms, forms + 2):
+                    forward(i)
+
             relay(forms, forms + 2)
-
-        @pl.when((n >= 1) & (n < 3))
-        def _():
-            low_d = 1 + (n - 1) * z_steps
-            lax.fori_loop(low_d, jnp.minimum(low_d + z_steps, size_ka), from_z, 0)
 
         @pl.when((n >= first_plane) & (n < first_plane + 4))
         def _():
@@ -494,31 +493,6 @@
         @pl.when(goes_down)
         def _():
             far_move(i, down_sem, below).wait_send()
-
-
-def hand_over_kernel(kernel, subspace, kernel_out, subspace_out, sems):
-    rows = kernel.shape[0] // COPIES
-    moves = [
-        pltpu.make_async_copy(
-            kernel.at[pl.ds(i * rows, rows)], kernel_out.at[pl.ds(i * rows, rows)], sems.at[i]
-        )
-        for i in range(COPIES)
-    ] + [pltpu.make_async_copy(subspace, subspace_out, sems.at[COPIES])]
-    for move in moves:
-        move.start()
-    for move in moves:
-        move.wait()
-
-
-def hand_over(kernel, subspace):
-    anywhere = pl.BlockSpec(memory_space=pl.ANY)
-    return pl.pallas_call(
-        hand_over_kernel,
-        out_shape=tuple(jax.ShapeDtypeStruct(x.shape, x.dtype) for x in (kernel, subspace)),
-        in_specs=[anywhere, anywhere],
-        out_specs=(anywhere, anywhere),
-        scratch_shapes=[pltpu.SemaphoreType.DMA((COPIES + 1,))],
-    )(kernel, subspace)
 
 
 def on_device(band_form, interp_coef, screen, coulomb, shift_map, grid_order, energies, initial):
@@ -575,7 +549,6 @@
         grid_order, band_form, interp_coef, screen.transpose(0, 2, 1), coulomb[None, :], shift_map,
         energies[None, :], initial.T,
     )
-    kernel, subspace = hand_over(kernel, subspace)
     return kernel, subspace.T
 
 

time: 96.6 us -> 82.6 us (0.86)
  Pallas kernels: 95.8 us -> 79.4 us
  local copies, waits for them, and re-layouts: 0 us -> 2.36 us
    pallas_call x1 -> x0, Pallas kernels: 13.1 us -> none  [hand_over(): pl.pallas_call(hand_over_kernel, out_shape=tuple((jax.ShapeDtypeStruct(x....]
    pallas_call x1, Pallas kernels: 82.7 us -> 79.4 us  [on_device(): pl.pallas_call(functools.partial(whole_kernel, size_ka, size_kp), out_sha...]
    unnamed x0 -> x4, local copies, waits for them, and re-layouts: none -> 2.36 us
where the time goes in v5:
time: 82.6 us; the launch traced here: 82.4 us
  Pallas kernels  79.4 us (96%)
  local copies, waits for them, and re-layouts  2.36 us (3%)
    pallas_call x1, Pallas kernels, on_device(): pl.pallas_call(functools.partial(whole_kernel, size_ka, size_kp), out_sha...  79.4 us
    unnamed x4, local copies, waits for them, and re-layouts  2.36 us

profile of v5, /device:TPU:0, one launch (start us, length us, event | category | flops | bytes accessed | tf_op | source)
XLA Modules:
  0.0 82.4 jit_solution(8602464639347675385)
XLA Ops:
  0.6 79.4 %shard_map.95 = (bf16[512,256]{1,0:T(8,128)(2,1)}, f32[64,512]{1,0:T(8,128)}) custom-call(s32[16]{0:T(128)} %grid_order.1, bf16[4,24,2048]{2,1,0:T(8,128)(2,1)} %form.1, bf16[4,128,128]{2,1,0:T(8,128)(2,1)} %coef.1, bf16[4,32,256]{2,1,0:T(8,128)(2,1)} %bitcast.7, f32[1,2048]{1,0:T(1,128)} %bitcast.8, s32[16,2048]{1,0:T(8,128)} %shift_map.1, ...), custom_call_target="tpu_custom_call" | custom-call | tf_op jit(solution)/shard_map/pallas_call | solution.py:510
  80.0 0.0 copy-start
  80.0 1.7 %copy.12 = bf16[512,256]{1,0:T(8,128)(2,1)} copy(bf16[512,256]{1,0:T(8,128)(2,1)} %get-tuple-element.8) | data formatting | bytes 524288
  81.7 0.0 copy-done
  81.8 0.7 copy.13
Async XLA Ops:
  80.0 1.7 %copy-start = (f32[64,512]{1,0:T(8,128)S(1)}, f32[64,512]{1,0:T(8,128)}, u32[]{:S(2)}) copy-start(f32[64,512]{1,0:T(8,128)} %get-tuple-element.5) | copy-start | bytes 393220

commit v6 on v5

--- a/solution.py
+++ b/solution.py
@@ -36,10 +36,14 @@
     work = jnp.where(lane == row + size, 1.0, work)
     for j in range(0, size, 2):
         first, second = work[j : j + 1, :], work[j + 1 : j + 2, :]
-        first_inverse = 1.0 / first[:, j : j + 1]
-        ratio = second[:, j : j + 1] * first_inverse
+        corner, above, beside, pivot = (
+            jnp.broadcast_to(line[:, at : at + 1], line.shape)
+            for line, at in ((first, j), (first, j + 1), (second, j), (second, j + 1))
+        )
+        first_inverse = 1.0 / corner
+        ratio = beside * first_inverse
         second = second - ratio * first
-        second_scaled = second * (1.0 / second[:, j + 1 : j + 2])
+        second_scaled = second * (1.0 / (pivot - ratio * above))
         first_scaled = first * first_inverse - ratio * second_scaled
         update = work[:, j : j + 1] * first_scaled + work[:, j + 1 : j + 2] * second_scaled
         work = jnp.where(row > j + 1, work - update, jnp.where(row == j + 1, second, work))

time: 82.6 us -> 79 us (0.956)
  Pallas kernels: 79.4 us -> 75.9 us
    pallas_call x1, Pallas kernels: 79.4 us -> 75.9 us  [on_device(): pl.pallas_call(functools.partial(whole_kernel, size_ka, size_kp), out_sha...]
where the time goes in v6:
time: 79 us; the launch traced here: 78.9 us
  Pallas kernels  75.9 us (96%)
  local copies, waits for them, and re-layouts  2.36 us (3%)
    pallas_call x1, Pallas kernels, on_device(): pl.pallas_call(functools.partial(whole_kernel, size_ka, size_kp), out_sha...  75.9 us
    unnamed x4, local copies, waits for them, and re-layouts  2.36 us

profile of v6, /device:TPU:0, one launch (start us, length us, event | category | flops | bytes accessed | tf_op | source)
XLA Modules:
  0.0 78.9 jit_solution(6217273073000797780)
XLA Ops:
  0.6 75.9 %shard_map.95 = (bf16[512,256]{1,0:T(8,128)(2,1)}, f32[64,512]{1,0:T(8,128)}) custom-call(s32[16]{0:T(128)} %grid_order.1, bf16[4,24,2048]{2,1,0:T(8,128)(2,1)} %form.1, bf16[4,128,128]{2,1,0:T(8,128)(2,1)} %coef.1, bf16[4,32,256]{2,1,0:T(8,128)(2,1)} %bitcast.7, f32[1,2048]{1,0:T(1,128)} %bitcast.8, s32[16,2048]{1,0:T(8,128)} %shift_map.1, ...), custom_call_target="tpu_custom_call" | custom-call | tf_op jit(solution)/shard_map/pallas_call | solution.py:514
  76.5 0.0 copy-start
  76.5 1.7 %copy.12 = bf16[512,256]{1,0:T(8,128)(2,1)} copy(bf16[512,256]{1,0:T(8,128)(2,1)} %get-tuple-element.8) | data formatting | bytes 524288
  78.2 0.0 copy-done
  78.2 0.7 copy.13
Async XLA Ops:
  76.5 1.7 %copy-start = (f32[64,512]{1,0:T(8,128)S(1)}, f32[64,512]{1,0:T(8,128)}, u32[]{:S(2)}) copy-start(f32[64,512]{1,0:T(8,128)} %get-tuple-element.5) | copy-start | bytes 393220
